TPU v7x, 256 devices: a whole 4x4x8 slice. The times are simulated.
256 devices in a mesh: seq: 64 (over z, x, core), grp: 4 (over y).
Axes of the slice: x: 4, y: 4, z: 8, core: 2. Of those that a mesh axis runs over, the one named last changes fastest.
Arguments:
- queries: bfloat16 [98304, 1024], P(('grp', 'seq')), parts along dimension 0, may hold values from -8 to 8
- keys: bfloat16 [98304, 1024], P(('grp', 'seq')), parts along dimension 0, may hold values from -8 to 8
- values: bfloat16 [98304, 1024], P(('grp', 'seq')), parts along dimension 0, may hold values from -6 to 6
- grad_out: bfloat16 [98304, 1024], P(('grp', 'seq')), parts along dimension 0, may hold values from -6 to 6
- cluster: int32 [8, 98304, 1], P(None, ('grp', 'seq')), parts along dimension 1, may hold values from 0 to 63; in each aligned block of 384 rows (0 to 383, 384 to 767, ..., all dimensions but the last counted through in order) at most 12 rows name the same one
Outputs:
- attn_out: bfloat16 [98304, 1024], P(('grp', 'seq')), parts along dimension 0
- grad_query: bfloat16 [98304, 1024], P(('grp', 'seq')), parts along dimension 0
- grad_key: bfloat16 [98304, 1024], P(('grp', 'seq')), parts along dimension 0
- grad_value: bfloat16 [98304, 1024], P(('grp', 'seq')), parts along dimension 0
There are 4 independent parts, one for each index of `grp`. A program takes and returns all parts, laid end to end along the dimension named above; each array names one. Nothing has to cross between parts.
Inputs may be any that keep to these rules, and one draw needn't show every extreme that they name: In each head, the 384 tokens of one device name one cluster at most 12 times.
All inputs are finite; a program needn't handle non-finite values.
Results may differ from a plain program's by a relative error of at most 0.017.
The roundings to bfloat16 on the way count: a program that leaves them out, or rounds other values in their place, can miss the bound.
Values may be sent and summed in bfloat16 or wider, within the bound.
A program may use at most 64 MiB of HBM per device.

v0:
```python
import jax
import jax.numpy as jnp
from jax import lax
from jax.sharding import PartitionSpec as P

CLUS_DEV = 1


def probabilities(query_slots, key_slots, valid_mask, score_scale):
    scores = (
        jnp.einsum("cid,cjd->cij", query_slots, key_slots, preferred_element_type=jnp.float32)
        * score_scale
    )
    ladder = jnp.arange(scores.shape[-1])
    allowed = (
        valid_mask[..., :, None] & valid_mask[..., None, :] & (ladder[None, :] <= ladder[:, None])
    )
    scores = jnp.where(allowed, scores, -1e30)
    largest = jnp.max(scores, axis=-1, keepdims=True)
    powered = jnp.exp(scores - largest)
    return powered / jnp.sum(powered, axis=-1, keepdims=True)


def attend(query_slots, key_slots, value_slots, valid_mask, score_scale):

    def attend_one_head(packed):
        query_one, key_one, value_one, mask_one = packed
        weights = probabilities(query_one, key_one, mask_one, score_scale)
        output_one = jnp.einsum(
            "cij,cjd->cid",
            weights.astype(jnp.bfloat16),
            value_one,
            preferred_element_type=jnp.float32,
        )
        return output_one.astype(jnp.bfloat16)

    return lax.map(attend_one_head, (query_slots, key_slots, value_slots, valid_mask))


def gradients(
    query_slots, key_slots, value_slots, valid_mask, output_slots, grad_slots, score_scale
):

    def gradients_one_head(packed):
        query_one, key_one, value_one, mask_one, output_one, grad_one = packed
        weights = probabilities(query_one, key_one, mask_one, score_scale)
        rounded = weights.astype(jnp.bfloat16)
        grad_value = jnp.einsum(
            "cij,cid->cjd", rounded, grad_one, preferred_element_type=jnp.float32
        ).astype(jnp.bfloat16)
        grad_weights = jnp.einsum(
            "cid,cjd->cij", grad_one, value_one, preferred_element_type=jnp.float32
        )
        row_dot = jnp.sum(
            grad_one.astype(jnp.float32) * output_one.astype(jnp.float32), axis=-1, keepdims=True
        )
        score_grad = (weights * (grad_weights - row_dot)).astype(jnp.bfloat16)
        grad_query = (
            jnp.einsum("cij,cjd->cid", score_grad, key_one, preferred_element_type=jnp.float32)
            * score_scale
        )
        grad_key = (
            jnp.einsum("cij,cid->cjd", score_grad, query_one, preferred_element_type=jnp.float32)
            * score_scale
        )
        return (grad_query.astype(jnp.bfloat16), grad_key.astype(jnp.bfloat16), grad_value)

    return lax.map(
        gradients_one_head,
        (query_slots, key_slots, value_slots, valid_mask, output_slots, grad_slots),
    )


def to_slots(block_in, owned_count):
    sender_count, head_count, slot_count, feature_width = block_in.shape
    per_cluster = slot_count // owned_count
    split_view = block_in.reshape(sender_count, head_count, owned_count, per_cluster, feature_width)
    return split_view.transpose(1, 2, 0, 3, 4).reshape(
        head_count, owned_count, sender_count * per_cluster, feature_width
    )


def back_slots(block_in, sender_count):
    head_count, owned_count, slot_count, feature_width = block_in.shape
    per_sender = slot_count // sender_count
    split_view = block_in.reshape(head_count, owned_count, sender_count, per_sender, feature_width)
    return split_view.transpose(0, 2, 1, 3, 4).reshape(
        head_count, sender_count, owned_count * per_sender, feature_width
    )


def slot_valid(tallies, slot_most):
    sender_count, head_count, owned_count = tallies.shape
    moved = tallies.transpose(1, 2, 0)
    valid_mask = moved[..., None] > jnp.arange(slot_most)[None, None, None, :]
    return valid_mask.reshape(head_count, owned_count, sender_count * slot_most)


def per_device(queries, keys, values, grad_out, cluster):
    seq_count = lax.axis_size("seq")
    row_count = queries.shape[0]
    head_count = cluster.shape[0]
    feature_width = queries.shape[1] // head_count
    owned_count = CLUS_DEV
    slot_most = 2 * row_count // (owned_count * seq_count)
    score_scale = feature_width ** (-0.5)
    labels = cluster[:, :, 0]
    places = jnp.arange(row_count)
    before = places[None, :] < places[:, None]
    ranking = jnp.sum((labels[:, :, None] == labels[:, None, :]) & before[None], axis=2)
    owners = (labels // owned_count).T
    inners = (labels % owned_count * slot_most + ranking).T
    head_ids = jnp.broadcast_to(
        jnp.arange(head_count, dtype=jnp.int32)[None, :], (row_count, head_count)
    )
    tallies = jnp.sum(
        labels[:, :, None] == jnp.arange(seq_count * owned_count, dtype=jnp.int32)[None, None, :],
        axis=1,
    )
    tallies = tallies.reshape(head_count, seq_count, owned_count).transpose(1, 0, 2)

    def pack(source):
        buffer = jnp.zeros(
            (seq_count, head_count, owned_count * slot_most, feature_width), source.dtype
        )
        return buffer.at[owners, head_ids, inners].set(
            source.reshape(row_count, head_count, feature_width)
        )

    def unpack(returned):
        return returned[head_ids, owners, inners].reshape(row_count, head_count * feature_width)

    query_buffer = pack(queries)
    key_buffer = pack(keys)
    value_buffer = pack(values)
    grad_buffer = pack(grad_out)
    query_in = lax.all_to_all(query_buffer, "seq", split_axis=0, concat_axis=0, tiled=True)
    key_in = lax.all_to_all(key_buffer, "seq", split_axis=0, concat_axis=0, tiled=True)
    value_in = lax.all_to_all(value_buffer, "seq", split_axis=0, concat_axis=0, tiled=True)
    tallies_in = lax.all_to_all(tallies, "seq", split_axis=0, concat_axis=0, tiled=True)
    query_slots = to_slots(query_in, owned_count)
    key_slots = to_slots(key_in, owned_count)
    value_slots = to_slots(value_in, owned_count)
    valid_mask = slot_valid(tallies_in, slot_most)
    output_slots = attend(query_slots, key_slots, value_slots, valid_mask, score_scale)
    output_back = lax.all_to_all(
        back_slots(output_slots, seq_count), "seq", split_axis=1, concat_axis=1, tiled=True
    )
    grad_in = lax.all_to_all(grad_buffer, "seq", split_axis=0, concat_axis=0, tiled=True)
    grad_slots = to_slots(grad_in, owned_count)
    grad_query, grad_key, grad_value = gradients(
        query_slots, key_slots, value_slots, valid_mask, output_slots, grad_slots, score_scale
    )
    grad_back = (
        lax.all_to_all(
            back_slots(grad_query, seq_count), "seq", split_axis=1, concat_axis=1, tiled=True
        ),
        lax.all_to_all(
            back_slots(grad_key, seq_count), "seq", split_axis=1, concat_axis=1, tiled=True
        ),
        lax.all_to_all(
            back_slots(grad_value, seq_count), "seq", split_axis=1, concat_axis=1, tiled=True
        ),
    )
    returned = (output_back, grad_back[0], grad_back[1], grad_back[2])
    return (unpack(returned[0]), unpack(returned[1]), unpack(returned[2]), unpack(returned[3]))


def solution(mesh):
    return jax.shard_map(
        per_device,
        mesh=mesh,
        in_specs=(
            P(("grp", "seq"), None),
            P(("grp", "seq"), None),
            P(("grp", "seq"), None),
            P(("grp", "seq"), None),
            P(None, ("grp", "seq"), None),
        ),
        out_specs=(
            P(("grp", "seq"), None),
            P(("grp", "seq"), None),
            P(("grp", "seq"), None),
            P(("grp", "seq"), None),
        ),
        check_vma=False,
    )
```

profile of v0, /device:TPU:1, one launch (start us, length us, event | category | flops | bytes accessed | tf_op | source)
XLA Modules:
  0.0 554.7 jit_solution(17768960806658478121)
XLA Ops:
  2.3 13.0 %all-to-all-start = ((s32[64,8,1]{1,2,0:T(1,128)}), s32[64,8,1]{1,2,0:T(1,128)S(1)}, u32[]{:S(2)}, u32[]{:S(2)}) async-start(s32[64,8,1]{1,2,0:T(1,128)} %copy.76), calls=%async_computation | async-start | bytes 65536 | tf_op jit(solution)/shard_map/all_to_all | solution.py:140
  19.8 9.6 %scatter_custom_fusion = bf16[6144,128]{1,0:T(8,128)(2,1)} fusion(s32[3072]{0:T(1024)S(1)} %reshape.325, bf16[3072,128]{1,0:T(8,128)(2,1)S(1)} %reshape.327, bf16[]{:T(256)} %constant.76.clone.1), kind=kCustom, calls=%fused_computation.75 | custom fusion | bytes 1572866
  29.5 10.4 %all-to-all-start.1 = ((bf16[64,8,12,128]{3,1,2,0:T(8,128)(2,1)}), bf16[64,8,12,128]{3,1,2,0:T(8,128)(2,1)S(1)}, u32[]{:S(2)}, u32[]{:S(2)}) async-start(bf16[64,8,12,128]{3,1,2,0:T(8,128)(2,1)} %bitcast.20), calls=%async_computation.1 | async-start | bytes 3145728 | tf_op jit(solution)/shard_map/all_to_all | solution.py:137
  40.3 9.7 %scatter_custom_fusion.1 = bf16[6144,128]{1,0:T(8,128)(2,1)} fusion(s32[3072]{0:T(1024)S(1)} %reshape.325, bf16[3072,128]{1,0:T(8,128)(2,1)S(1)} %reshape.333, bf16[]{:T(256)} %constant.76.clone.1), kind=kCustom, calls=%fused_computation.73 | custom fusion | bytes 1572866
  49.9 29.0 %all-to-all-done.1 = bf16[64,8,12,128]{3,1,2,0:T(8,128)(2,1)S(1)} async-done(((bf16[64,8,12,128]{3,1,2,0:T(8,128)(2,1)}), bf16[64,8,12,128]{3,1,2,0:T(8,128)(2,1)S(1)}, u32[]{:S(2)}, u32[]{:S(2)}) %all-to-all-start.1) | async-done | bytes 1572896 | tf_op jit(solution)/shard_map/all_to_all | solution.py:137
  78.9 6.5 %all-to-all-start.2 = ((bf16[64,8,12,128]{3,1,2,0:T(8,128)(2,1)}), bf16[64,8,12,128]{3,1,2,0:T(8,128)(2,1)S(1)}, u32[]{:S(2)}, u32[]{:S(2)}) async-start(bf16[64,8,12,128]{3,1,2,0:T(8,128)(2,1)} %bitcast.154), calls=%async_computation.2 | async-start | bytes 3145728 | tf_op jit(solution)/shard_map/all_to_all | solution.py:138
  87.5 10.0 %scatter_custom_fusion.2 = bf16[6144,128]{1,0:T(8,128)(2,1)} fusion(s32[3072]{0:T(1024)S(1)} %reshape.325, bf16[3072,128]{1,0:T(8,128)(2,1)} %reshape.339, bf16[]{:T(256)} %constant.76.clone.1), kind=kCustom, calls=%fused_computation.71 | custom fusion | bytes 1573376
  97.5 26.9 %all-to-all-done.2 = bf16[64,8,12,128]{3,1,2,0:T(8,128)(2,1)S(1)} async-done(((bf16[64,8,12,128]{3,1,2,0:T(8,128)(2,1)}), bf16[64,8,12,128]{3,1,2,0:T(8,128)(2,1)S(1)}, u32[]{:S(2)}, u32[]{:S(2)}) %all-to-all-start.2) | async-done | bytes 1572896 | tf_op jit(solution)/shard_map/all_to_all | solution.py:138
  124.4 18.5 %all-to-all-start.3 = ((bf16[64,8,12,128]{3,1,2,0:T(8,128)(2,1)}), bf16[64,8,12,128]{3,1,2,0:T(8,128)(2,1)}, u32[]{:S(2)}, u32[]{:S(2)}) async-start(bf16[64,8,12,128]{3,1,2,0:T(8,128)(2,1)} %bitcast.152), calls=%async_computation.3 | async-start | bytes 3145728 | tf_op jit(solution)/shard_map/all_to_all | solution.py:139
  143.0 2.2 reshape.345
  145.1 10.0 %scatter_custom_fusion.3 = bf16[6144,128]{1,0:T(8,128)(2,1)} fusion(s32[3072]{0:T(1024)S(1)} %reshape.325, bf16[3072,128]{1,0:T(8,128)(2,1)} %reshape.345, bf16[]{:T(256)} %constant.76.clone.1), kind=kCustom, calls=%fused_computation.69 | custom fusion | bytes 1573376
  158.3 23.5 %all-to-all-done.3 = bf16[64,8,12,128]{3,1,2,0:T(8,128)(2,1)} async-done(((bf16[64,8,12,128]{3,1,2,0:T(8,128)(2,1)}), bf16[64,8,12,128]{3,1,2,0:T(8,128)(2,1)}, u32[]{:S(2)}, u32[]{:S(2)}) %all-to-all-start.3) | async-done | bytes 1572896 | tf_op jit(solution)/shard_map/all_to_all | solution.py:139
  181.8 6.5 %all-to-all-start.5 = ((bf16[64,8,12,128]{3,1,2,0:T(8,128)(2,1)}), bf16[64,8,12,128]{3,1,2,0:T(8,128)(2,1)S(1)}, u32[]{:S(2)}, u32[]{:S(2)}) async-start(bf16[64,8,12,128]{3,1,2,0:T(8,128)(2,1)} %bitcast.40), calls=%async_computation.5 | async-start | bytes 3145728 | tf_op jit(solution)/shard_map/all_to_all | solution.py:149
  188.3 2.7 copy.82
  191.2 28.5 %while.24 = (s32[]{:T(128)}, bf16[8,1,768,128]{3,2,1,0:T(8,128)(2,1)S(1)}, pred[8,1,768]{2,1,0:T(4,128)(4,1)S(1)}, bf16[8,1,768,128]{3,2,1,0:T(8,128)(2,1)}, bf1...) while((s32[]{:T(128)}, bf16[8,1,768,128]{3,2,1,0:T(8,128)(2,1)S(1)}, ...), condition=%wide.region_8.9_spmd, body=%wide.region_5.8_spmd.sunk | while | flops 308574720 | bytes 7887441 | solution.py:37
  219.7 7.5 %all-to-all-done.5 = bf16[64,8,12,128]{3,1,2,0:T(8,128)(2,1)S(1)} async-done(((bf16[64,8,12,128]{3,1,2,0:T(8,128)(2,1)}), bf16[64,8,12,128]{3,1,2,0:T(8,128)(2,1)S(1)}, u32[]{:S(2)}, u32[]{:S(2)}) %all-to-all-start.5) | async-done | bytes 1572896 | tf_op jit(solution)/shard_map/all_to_all | solution.py:149
  231.7 84.2 %while.25 = (s32[]{:T(128)}, bf16[8,1,768,128]{3,2,1,0:T(8,128)(2,1)S(1)}, bf16[8,1,768,128]{3,2,1,0:T(8,128)(2,1)}, bf16[8,1,768,128]{3,2,1,0:T(8,128)(2,1)}, p...) while((s32[]{:T(128)}, ...), condition=%wide.region_14.15_spmd, body=%wide.region_10.14_spmd.sunk | while | flops 765294336 | bytes 15371893 | solution.py:68
  254.7 2.2 fusion.101
  315.9 4.1 copy.93
  320.0 6.5 %all-to-all-start.7 = ((bf16[8,64,12,128]{3,0,2,1:T(8,128)(2,1)}), bf16[8,64,12,128]{3,0,2,1:T(8,128)(2,1)S(1)}, u32[]{:S(2)}, u32[]{:S(2)}) async-start(bf16[8,64,12,128]{3,0,2,1:T(8,128)(2,1)} %bitcast.157), calls=%async_computation.7 | async-start | bytes 3145728 | tf_op jit(solution)/shard_map/all_to_all | solution.py:158
  326.5 3.6 copy.95
  330.1 35.4 %all-to-all-done.7 = bf16[8,64,12,128]{3,0,2,1:T(8,128)(2,1)S(1)} async-done(((bf16[8,64,12,128]{3,0,2,1:T(8,128)(2,1)}), bf16[8,64,12,128]{3,0,2,1:T(8,128)(2,1)S(1)}, u32[]{:S(2)}, u32[]{:S(2)}) %all-to-all-start.7) | async-done | bytes 1572896 | tf_op jit(solution)/shard_map/all_to_all | solution.py:158
  365.5 6.6 %all-to-all-start.8 = ((bf16[8,64,12,128]{3,0,2,1:T(8,128)(2,1)}), bf16[8,64,12,128]{3,0,2,1:T(8,128)(2,1)}, u32[]{:S(2)}, u32[]{:S(2)}) async-start(bf16[8,64,12,128]{3,0,2,1:T(8,128)(2,1)} %bitcast.155), calls=%async_computation.8 | async-start | bytes 3145728 | tf_op jit(solution)/shard_map/all_to_all | solution.py:161
  372.1 3.6 copy.91
  375.7 35.3 %all-to-all-done.8 = bf16[8,64,12,128]{3,0,2,1:T(8,128)(2,1)} async-done(((bf16[8,64,12,128]{3,0,2,1:T(8,128)(2,1)}), bf16[8,64,12,128]{3,0,2,1:T(8,128)(2,1)}, u32[]{:S(2)}, u32[]{:S(2)}) %all-to-all-start.8) | async-done | bytes 1572896 | tf_op jit(solution)/shard_map/all_to_all | solution.py:161
  411.1 6.6 %all-to-all-start.6 = ((bf16[8,64,12,128]{3,0,2,1:T(8,128)(2,1)}), bf16[8,64,12,128]{3,0,2,1:T(8,128)(2,1)}, u32[]{:S(2)}, u32[]{:S(2)}) async-start(bf16[8,64,12,128]{3,0,2,1:T(8,128)(2,1)} %bitcast.156), calls=%async_computation.6 | async-start | bytes 3145728 | tf_op jit(solution)/shard_map/all_to_all | solution.py:155
  419.9 36.9 %all-to-all-done.6 = bf16[8,64,12,128]{3,0,2,1:T(8,128)(2,1)} async-done(((bf16[8,64,12,128]{3,0,2,1:T(8,128)(2,1)}), bf16[8,64,12,128]{3,0,2,1:T(8,128)(2,1)}, u32[]{:S(2)}, u32[]{:S(2)}) %all-to-all-start.6) | async-done | bytes 1572896 | tf_op jit(solution)/shard_map/all_to_all | solution.py:155
  456.8 6.8 %all-to-all-start.4 = ((bf16[8,64,12,128]{3,0,2,1:T(8,128)(2,1)}), bf16[8,64,12,128]{3,0,2,1:T(8,128)(2,1)}, u32[]{:S(2)}, u32[]{:S(2)}) async-start(bf16[8,64,12,128]{3,0,2,1:T(8,128)(2,1)} %bitcast.153), calls=%async_computation.4 | async-start | bytes 3145728 | tf_op jit(solution)/shard_map/all_to_all | solution.py:146
  464.5 19.7 %gather_fusion.2 = bf16[3072,128]{1,0:T(8,128)(2,1)S(1)} fusion(bf16[8,64,12,128]{3,1,2,0:T(8,128)(2,1)S(1)} %copy.94, s32[3072]{0:T(1024)S(1)} %reshape.301), kind=kCustom, calls=%fused_computation.2 | custom fusion | bytes 1609728 | tf_op jit(solution)/shard_map/gather | solution.py:131
  487.4 19.7 %gather_fusion.3 = bf16[3072,128]{1,0:T(8,128)(2,1)S(1)} fusion(bf16[8,64,12,128]{3,1,2,0:T(8,128)(2,1)S(1)} %copy.96, s32[3072]{0:T(1024)S(1)} %reshape.301), kind=kCustom, calls=%fused_computation.3 | custom fusion | bytes 1609728 | tf_op jit(solution)/shard_map/gather | solution.py:131
  510.4 19.7 %gather_fusion.1 = bf16[3072,128]{1,0:T(8,128)(2,1)S(1)} fusion(bf16[8,64,12,128]{3,1,2,0:T(8,128)(2,1)S(1)} %copy.92, s32[3072]{0:T(1024)S(1)} %reshape.301), kind=kCustom, calls=%fused_computation.1 | custom fusion | bytes 1609728 | tf_op jit(solution)/shard_map/gather | solution.py:131
  533.3 19.7 %gather_fusion = bf16[3072,128]{1,0:T(8,128)(2,1)S(1)} fusion(bf16[8,64,12,128]{3,1,2,0:T(8,128)(2,1)S(1)} %copy.85, s32[3072]{0:T(1024)S(1)} %reshape.301), kind=kCustom, calls=%fused_computation | custom fusion | bytes 1609728 | tf_op jit(solution)/shard_map/gather | solution.py:131
  (147 shorter events, 140.6 us)
Async XLA Ops:
  0.6 18.8 %copy-start.1 = (bf16[384,1024]{1,0:T(8,128)(2,1)S(1)}, bf16[384,1024]{1,0:T(8,128)(2,1)}, u32[]{:S(2)}) copy-start(bf16[384,1024]{1,0:T(8,128)(2,1)} %param.9) | copy-start | bytes 2359300
  2.3 27.1 %all-to-all-start = ((s32[64,8,1]{1,2,0:T(1,128)}), s32[64,8,1]{1,2,0:T(1,128)S(1)}, u32[]{:S(2)}, u32[]{:S(2)}) async-start(s32[64,8,1]{1,2,0:T(1,128)} %copy.76), calls=%async_computation | async-start | bytes 65536 | tf_op jit(solution)/shard_map/all_to_all | solution.py:140
  29.5 10.4 %copy-start.2 = (bf16[384,1024]{1,0:T(8,128)(2,1)S(1)}, bf16[384,1024]{1,0:T(8,128)(2,1)}, u32[]{:S(2)}) copy-start(bf16[384,1024]{1,0:T(8,128)(2,1)} %param.10) | copy-start | bytes 2359300
  29.5 49.4 %all-to-all-start.1 = ((bf16[64,8,12,128]{3,1,2,0:T(8,128)(2,1)}), bf16[64,8,12,128]{3,1,2,0:T(8,128)(2,1)S(1)}, u32[]{:S(2)}, u32[]{:S(2)}) async-start(bf16[64,8,12,128]{3,1,2,0:T(8,128)(2,1)} %bitcast.20), calls=%async_computation.1 | async-start | bytes 3145728 | tf_op jit(solution)/shard_map/all_to_all | solution.py:137
  78.9 45.5 %all-to-all-start.2 = ((bf16[64,8,12,128]{3,1,2,0:T(8,128)(2,1)}), bf16[64,8,12,128]{3,1,2,0:T(8,128)(2,1)S(1)}, u32[]{:S(2)}, u32[]{:S(2)}) async-start(bf16[64,8,12,128]{3,1,2,0:T(8,128)(2,1)} %bitcast.154), calls=%async_computation.2 | async-start | bytes 3145728 | tf_op jit(solution)/shard_map/all_to_all | solution.py:138
  124.4 57.4 %all-to-all-start.3 = ((bf16[64,8,12,128]{3,1,2,0:T(8,128)(2,1)}), bf16[64,8,12,128]{3,1,2,0:T(8,128)(2,1)}, u32[]{:S(2)}, u32[]{:S(2)}) async-start(bf16[64,8,12,128]{3,1,2,0:T(8,128)(2,1)} %bitcast.152), calls=%async_computation.3 | async-start | bytes 3145728 | tf_op jit(solution)/shard_map/all_to_all | solution.py:139
  181.8 45.5 %all-to-all-start.5 = ((bf16[64,8,12,128]{3,1,2,0:T(8,128)(2,1)}), bf16[64,8,12,128]{3,1,2,0:T(8,128)(2,1)S(1)}, u32[]{:S(2)}, u32[]{:S(2)}) async-start(bf16[64,8,12,128]{3,1,2,0:T(8,128)(2,1)} %bitcast.40), calls=%async_computation.5 | async-start | bytes 3145728 | tf_op jit(solution)/shard_map/all_to_all | solution.py:149
  315.9 4.2 copy-start
  320.0 45.5 %all-to-all-start.7 = ((bf16[8,64,12,128]{3,0,2,1:T(8,128)(2,1)}), bf16[8,64,12,128]{3,0,2,1:T(8,128)(2,1)S(1)}, u32[]{:S(2)}, u32[]{:S(2)}) async-start(bf16[8,64,12,128]{3,0,2,1:T(8,128)(2,1)} %bitcast.157), calls=%async_computation.7 | async-start | bytes 3145728 | tf_op jit(solution)/shard_map/all_to_all | solution.py:158
  365.5 45.6 %all-to-all-start.8 = ((bf16[8,64,12,128]{3,0,2,1:T(8,128)(2,1)}), bf16[8,64,12,128]{3,0,2,1:T(8,128)(2,1)}, u32[]{:S(2)}, u32[]{:S(2)}) async-start(bf16[8,64,12,128]{3,0,2,1:T(8,128)(2,1)} %bitcast.155), calls=%async_computation.8 | async-start | bytes 3145728 | tf_op jit(solution)/shard_map/all_to_all | solution.py:161
  411.1 45.7 %all-to-all-start.6 = ((bf16[8,64,12,128]{3,0,2,1:T(8,128)(2,1)}), bf16[8,64,12,128]{3,0,2,1:T(8,128)(2,1)}, u32[]{:S(2)}, u32[]{:S(2)}) async-start(bf16[8,64,12,128]{3,0,2,1:T(8,128)(2,1)} %bitcast.156), calls=%async_computation.6 | async-start | bytes 3145728 | tf_op jit(solution)/shard_map/all_to_all | solution.py:155
  456.8 6.8 %copy-start.3 = (s32[8,384,1]{1,2,0:T(1,128)S(1)}, s32[8,384,1]{1,2,0:T(1,128)}, u32[]{:S(2)}) copy-start(s32[8,384,1]{1,2,0:T(1,128)} %param.13) | copy-start | bytes 36868
  456.8 74.5 %all-to-all-start.4 = ((bf16[8,64,12,128]{3,0,2,1:T(8,128)(2,1)}), bf16[8,64,12,128]{3,0,2,1:T(8,128)(2,1)}, u32[]{:S(2)}, u32[]{:S(2)}) async-start(bf16[8,64,12,128]{3,0,2,1:T(8,128)(2,1)} %bitcast.153), calls=%async_computation.4 | async-start | bytes 3145728 | tf_op jit(solution)/shard_map/all_to_all | solution.py:146
where the time goes:
time: 566 us; the launch traced here: 555 us
  waiting for transfers between devices  195 us (34%)
  local copies, waits for them, and re-layouts  161 us (28%)
  matrix products  97.1 us (17%)
  starting transfers between devices  81.3 us (14%)
  other arithmetic  18.8 us (3%)
    gather x4, local copies, waits for them, and re-layouts, unpack(): returned[head_ids, owners, inners]  78.9 us
    unnamed x15, local copies, waits for them, and re-layouts  40.3 us
    all_to_all x1, waiting for transfers between devices, per_device(): lax.all_to_all(back_slots(grad_query, seq_count), 'seq', split_axis=1, co...  36.9 us
    all_to_all x1, waiting for transfers between devices, per_device(): lax.all_to_all(back_slots(grad_key, seq_count), 'seq', split_axis=1, conc...  35.4 us
    all_to_all x1, waiting for transfers between devices, per_device(): lax.all_to_all(back_slots(grad_value, seq_count), 'seq', split_axis=1, co...  35.3 us
    all_to_all x1, waiting for transfers between devices, per_device(): lax.all_to_all(query_buffer, 'seq', split_axis=0, concat_axis=0, tiled=True)  29 us
    all_to_all x1, waiting for transfers between devices, per_device(): lax.all_to_all(key_buffer, 'seq', split_axis=0, concat_axis=0, tiled=True)  26.9 us
    dot_general x16, matrix products, probabilities(): jnp.einsum('cid,cjd->cij', query_slots, key_slots, preferred_element_type...  25.1 us
  transfers between devices with their start and end apart: 9, of which 7 were waited for; matrix products, arithmetic and copies ran while one was open for 29% of the time, Pallas kernels for 0%

commit v1 on v0

v1 whole, which is shorter than its diff:
```python
import functools

import jax
import jax.numpy as jnp
import numpy as np
from jax import lax
from jax.experimental import pallas as pl
from jax.experimental.pallas import tpu as pltpu
from jax.sharding import PartitionSpec as P

MESH = pl.DeviceIdType.MESH
HEADS = 8
DIM = 128
ROWS = 384
CLUSTERS = 64
MOST = 12
LINE = 8
OWNED = 8
PIECE = OWNED * MOST
SLOTS = LINE * PIECE
CAP = LINE * LINE * MOST
HALF = SLOTS // 2
ABSENT = 64.0
NEG = -1e30
VMEM = pltpu.VMEM
ANY = pl.ANY


def place(i):
    return jnp.where(i % 2 == 1, (i + 1) // 2, (LINE - i // 2) % LINE)


def greet(z, r):
    barrier = pltpu.get_barrier_semaphore()
    for i in range(1, LINE):
        pl.semaphore_signal(
            barrier, inc=1, device_id={"seq": lax.rem(z + i, LINE) * LINE + r}, device_id_type=MESH
        )
        pl.semaphore_signal(
            barrier, inc=1, device_id={"seq": z * LINE + lax.rem(r + i, LINE)}, device_id_type=MESH
        )
    pl.semaphore_wait(barrier, 2 * (LINE - 1))


def wait_for(ref, sem):
    pltpu.make_async_copy(ref, ref, sem).wait()


def piece(o):
    return pl.ds(pl.multiple_of(o * PIECE, PIECE), PIECE)


def lanes(h):
    return pl.ds(pl.multiple_of(h * DIM, DIM), DIM)


def gather_kernel(
    q_ref, k_ref, v_ref, g_ref, label_ref, order_ref,
    out_ref, slot_ref,
    zbuf, zlab, xsrc, xbuf, z_send, z_recv, l_send, l_recv, x_send, x_recv,
):
    me = lax.axis_index("seq")
    z, r = me // LINE, me % LINE
    sources = (q_ref, k_ref, v_ref, g_ref)
    greet(z, r)

    def send_z(i, _):
        to = (z + place(i)) % LINE
        peer = {"seq": to * LINE + r}
        pltpu.make_async_remote_copy(
            src_ref=label_ref.at[to], dst_ref=zlab.at[z], send_sem=l_send, recv_sem=l_recv.at[z],
            device_id=peer, device_id_type=MESH,
        ).start()
        for a in range(4):
            pltpu.make_async_remote_copy(
                src_ref=sources[a].at[:, lanes(to)], dst_ref=zbuf.at[z, a],
                send_sem=z_send.at[i], recv_sem=z_recv.at[z],
                device_id=peer, device_id_type=MESH,
            ).start()
        return 0

    pltpu.make_async_copy(label_ref.at[z], zlab.at[z], l_recv.at[z]).start()
    for a in range(4):
        pltpu.make_async_copy(
            sources[a].at[:, lanes(z)], zbuf.at[z, a], z_recv.at[z]
        ).start()
    lax.fori_loop(1, LINE, send_z, 0)

    before = (
        lax.broadcasted_iota(jnp.int32, (ROWS, ROWS), 0)
        < lax.broadcasted_iota(jnp.int32, (ROWS, ROWS), 1)
    ).astype(jnp.float32).astype(jnp.bfloat16)

    def regroup(s):
        wait_for(xbuf.at[s], x_recv.at[s])
        for half in range(2):
            moved = jnp.dot(
                order_ref[...], xbuf[s, half * HALF:(half + 1) * HALF],
                preferred_element_type=jnp.float32,
            ).astype(jnp.bfloat16)
            for j in range(OWNED):
                at = pl.multiple_of(s * PIECE + half * 48, 16)
                out_ref[j, pl.ds(at, 48), :] = moved[j * 48:(j + 1) * 48]

    def step(i, _):
        s = (z - place(i) + LINE) % LINE
        wait_for(zlab.at[s], l_recv.at[s])
        label = zlab[s]
        named = (
            lax.broadcasted_iota(jnp.int32, (CLUSTERS, ROWS), 0) == label
        ).astype(jnp.float32)
        earlier = jnp.dot(
            named.astype(jnp.bfloat16), before, preferred_element_type=jnp.float32
        )
        rank = jnp.sum(named * earlier, axis=0, keepdims=True)
        slot = label * MOST + rank.astype(jnp.int32)
        slot_ref[s] = slot
        pick = (
            lax.broadcasted_iota(jnp.int32, (SLOTS, ROWS), 0) == slot
        ).astype(jnp.float32)
        used = jnp.sum(pick, axis=1, keepdims=True)
        mark = jnp.where(
            lax.broadcasted_iota(jnp.int32, (SLOTS, DIM), 1) == 0, (1.0 - used) * ABSENT, 0.0
        )
        pick = pick.astype(jnp.bfloat16)
        wait_for(zbuf.at[s], z_recv.at[s])
        for a in range(4):
            packed = jnp.dot(pick, zbuf[s, a], preferred_element_type=jnp.float32)
            if a == 1:
                packed = packed + mark
            xsrc[s, :, a * DIM:(a + 1) * DIM] = packed.astype(jnp.bfloat16)
        pltpu.make_async_copy(xsrc.at[s, piece(r)], xbuf.at[s, piece(r)], x_recv.at[s]).start()

        def send_x(n, _):
            o = (r + n) % LINE
            pltpu.make_async_remote_copy(
                src_ref=xsrc.at[s, piece(o)], dst_ref=xbuf.at[s, piece(r)],
                send_sem=x_send.at[s], recv_sem=x_recv.at[s],
                device_id={"seq": z * LINE + o}, device_id_type=MESH,
            ).start()
            return 0

        lax.fori_loop(1, LINE, send_x, 0)

        @pl.when(i > 0)
        def _():
            regroup((z - place(i - 1) + LINE) % LINE)

        return 0

    lax.fori_loop(0, LINE, step, 0)
    regroup((z - place(LINE - 1) + LINE) % LINE)

    def drain(i, _):
        wait_for(xsrc.at[i, pl.ds(0, SLOTS - PIECE)], x_send.at[i])

        @pl.when(i > 0)
        def _():
            wait_for(zbuf.at[i], z_send.at[i])
            wait_for(zlab.at[i], l_send)

        return 0

    lax.fori_loop(0, LINE, drain, 0)


def attend_kernel(x_ref, out_ref, dk_acc, dv_acc):
    scale = DIM ** -0.5
    block = 256
    k_all = x_ref[0, :, DIM:2 * DIM]
    v_all = x_ref[0, :, 2 * DIM:3 * DIM]
    first = (lax.broadcasted_iota(jnp.int32, (8, DIM), 1) == 0).astype(jnp.float32).astype(jnp.bfloat16)
    marks = lax.dot_general(
        first, k_all, (((1,), (1,)), ((), ())), preferred_element_type=jnp.float32
    )[0:1]
    bias = jnp.where(marks > ABSENT / 2, NEG, 0.0)
    for b in range(CAP // block):
        lo, hi = b * block, (b + 1) * block
        q = x_ref[0, lo:hi, 0:DIM]
        g = x_ref[0, lo:hi, 3 * DIM:4 * DIM]
        k, v = k_all[:hi], v_all[:hi]
        scores = lax.dot_general(
            q, k, (((1,), (1,)), ((), ())), preferred_element_type=jnp.float32
        ) * scale
        scores = scores + bias[:, :hi]
        late = (
            lax.broadcasted_iota(jnp.int32, (block, hi), 1)
            > lax.broadcasted_iota(jnp.int32, (block, hi), 0) + lo
        )
        scores = jnp.where(late, NEG, scores)
        powered = jnp.exp(scores - jnp.max(scores, axis=-1, keepdims=True))
        weights = powered * (1.0 / jnp.sum(powered, axis=-1, keepdims=True))
        rounded = weights.astype(jnp.bfloat16)
        o = jnp.dot(rounded, v, preferred_element_type=jnp.float32).astype(jnp.bfloat16)
        out_ref[0, lo:hi, 0:DIM] = o
        dv = lax.dot_general(
            rounded, g, (((0,), (0,)), ((), ())), preferred_element_type=jnp.float32
        )
        grad_weights = lax.dot_general(
            g, v, (((1,), (1,)), ((), ())), preferred_element_type=jnp.float32
        )
        row_dot = jnp.sum(
            g.astype(jnp.float32) * o.astype(jnp.float32), axis=-1, keepdims=True
        )
        ds = (weights * (grad_weights - row_dot)).astype(jnp.bfloat16)
        dq = jnp.dot(ds, k, preferred_element_type=jnp.float32) * scale
        out_ref[0, lo:hi, DIM:2 * DIM] = dq.astype(jnp.bfloat16)
        dk = lax.dot_general(
            ds, q, (((0,), (0,)), ((), ())), preferred_element_type=jnp.float32
        )
        if b == 0:
            dk_acc[lo:hi], dv_acc[lo:hi] = dk, dv
        else:
            dk_acc[:lo] += dk[:lo]
            dv_acc[:lo] += dv[:lo]
            dk_acc[lo:hi], dv_acc[lo:hi] = dk[lo:], dv[lo:]
    out_ref[0, :, 2 * DIM:3 * DIM] = (dk_acc[...] * scale).astype(jnp.bfloat16)
    out_ref[0, :, 3 * DIM:4 * DIM] = dv_acc[...].astype(jnp.bfloat16)


def return_kernel(
    y_ref, slot_ref, order_ref,
    o_ref, dq_ref, dk_ref, dv_ref,
    xsrc, xbuf, zsrc, x_send, x_recv, z_send, z_recv,
):
    me = lax.axis_index("seq")
    z, r = me // LINE, me % LINE
    results = (o_ref, dq_ref, dk_ref, dv_ref)
    greet(z, r)

    def spread(i):
        s = (z + place(i)) % LINE
        for half in range(2):
            at = pl.multiple_of(s * PIECE + half * 48, 16)
            taken = jnp.concatenate([y_ref[j, pl.ds(at, 48), :] for j in range(OWNED)], axis=0)
            xsrc[s, half * HALF:(half + 1) * HALF] = jnp.dot(
                order_ref[...], taken, preferred_element_type=jnp.float32
            ).astype(jnp.bfloat16)
        pltpu.make_async_copy(xsrc.at[s, piece(r)], xbuf.at[s, piece(r)], x_recv.at[s]).start()

        def send_x(n, _):
            o = (r + n) % LINE
            pltpu.make_async_remote_copy(
                src_ref=xsrc.at[s, piece(o)], dst_ref=xbuf.at[s, piece(r)],
                send_sem=x_send.at[s], recv_sem=x_recv.at[s],
                device_id={"seq": z * LINE + o}, device_id_type=MESH,
            ).start()
            return 0

        lax.fori_loop(1, LINE, send_x, 0)

    def deliver(i, own):
        s = (z + place(i)) % LINE
        wide = jnp.broadcast_to(slot_ref[s].astype(jnp.float32), (DIM, ROWS))
        column = wide.T[:, 0:1].astype(jnp.int32)
        pick = (
            lax.broadcasted_iota(jnp.int32, (ROWS, SLOTS), 1) == column
        ).astype(jnp.float32).astype(jnp.bfloat16)
        wait_for(xbuf.at[s], x_recv.at[s])
        for a in range(4):
            zsrc[s, a] = jnp.dot(
                pick, xbuf[s, :, a * DIM:(a + 1) * DIM], preferred_element_type=jnp.float32
            ).astype(jnp.bfloat16)
        for a in range(4):
            if own:
                pltpu.make_async_copy(
                    zsrc.at[s, a], results[a].at[:, lanes(z)], z_recv.at[z]
                ).start()
            else:
                pltpu.make_async_remote_copy(
                    src_ref=zsrc.at[s, a], dst_ref=results[a].at[:, lanes(z)],
                    send_sem=z_send.at[s], recv_sem=z_recv.at[z],
                    device_id={"seq": s * LINE + r}, device_id_type=MESH,
                ).start()

    spread(0)
    spread(1)
    deliver(0, True)

    def step(i, _):
        spread(i + 1)
        deliver(i, False)
        return 0

    lax.fori_loop(1, LINE - 1, step, 0)
    deliver(LINE - 1, False)

    def drain(i, _):
        wait_for(xsrc.at[i, pl.ds(0, SLOTS - PIECE)], x_send.at[i])
        wait_for(zsrc.at[i], z_recv.at[i])

        @pl.when(i != z)
        def _():
            wait_for(zsrc.at[i], z_send.at[i])

        return 0

    lax.fori_loop(0, LINE, drain, 0)


def regroup_order():
    out = np.arange(HALF)
    source = (out % 48) // MOST * PIECE + out // 48 * MOST + out % MOST
    return (np.arange(HALF)[None, :] == source[:, None]).astype(np.float32)


def per_device(queries, keys, values, grad_out, cluster):
    dma = pltpu.SemaphoreType.DMA
    bf16 = jnp.bfloat16
    labels = cluster.reshape(HEADS, 1, ROWS)
    order = jnp.asarray(regroup_order(), bf16)
    slots, numbers = pl.pallas_call(
        gather_kernel,
        out_shape=(
            jax.ShapeDtypeStruct((OWNED, CAP, 4 * DIM), bf16),
            jax.ShapeDtypeStruct((LINE, 1, ROWS), jnp.int32),
        ),
        in_specs=[pl.BlockSpec(memory_space=ANY)] * 4 + [pl.BlockSpec(memory_space=VMEM)] * 2,
        out_specs=[pl.BlockSpec(memory_space=VMEM)] * 2,
        scratch_shapes=[
            VMEM((LINE, 4, ROWS, DIM), bf16),
            VMEM((LINE, 1, ROWS), jnp.int32),
            VMEM((LINE, SLOTS, 4 * DIM), bf16),
            VMEM((LINE, SLOTS, 4 * DIM), bf16),
            dma((LINE,)), dma((LINE,)), dma, dma((LINE,)), dma((LINE,)), dma((LINE,)),
        ],
        compiler_params=pltpu.CompilerParams(
            collective_id=0, has_side_effects=True, vmem_limit_bytes=56 * 2**20
        ),
        name="gather",
    )(queries, keys, values, grad_out, labels, order)
    results = pl.pallas_call(
        attend_kernel,
        grid=(OWNED,),
        out_shape=jax.ShapeDtypeStruct((OWNED, CAP, 4 * DIM), bf16),
        in_specs=[pl.BlockSpec((1, CAP, 4 * DIM), lambda j: (j, 0, 0))],
        out_specs=pl.BlockSpec((1, CAP, 4 * DIM), lambda j: (j, 0, 0)),
        scratch_shapes=[VMEM((CAP, DIM), jnp.float32), VMEM((CAP, DIM), jnp.float32)],
        compiler_params=pltpu.CompilerParams(vmem_limit_bytes=48 * 2**20),
        name="attend",
    )(slots)
    return pl.pallas_call(
        return_kernel,
        out_shape=[jax.ShapeDtypeStruct((ROWS, HEADS * DIM), bf16)] * 4,
        in_specs=[pl.BlockSpec(memory_space=VMEM)] * 3,
        out_specs=[pl.BlockSpec(memory_space=ANY)] * 4,
        scratch_shapes=[
            VMEM((LINE, SLOTS, 4 * DIM), bf16),
            VMEM((LINE, SLOTS, 4 * DIM), bf16),
            VMEM((LINE, 4, ROWS, DIM), bf16),
            dma((LINE,)), dma((LINE,)), dma((LINE,)), dma((LINE,)),
        ],
        compiler_params=pltpu.CompilerParams(
            collective_id=1, has_side_effects=True, vmem_limit_bytes=56 * 2**20
        ),
        name="return",
    )(results, numbers, order.T)


def solution(mesh):
    return jax.shard_map(
        per_device,
        mesh=mesh,
        in_specs=(
            P(("grp", "seq"), None),
            P(("grp", "seq"), None),
            P(("grp", "seq"), None),
            P(("grp", "seq"), None),
            P(None, ("grp", "seq"), None),
        ),
        out_specs=(P(("grp", "seq"), None),) * 4,
        check_vma=False,
    )
```

time: 566 us -> 241 us (0.43)
  the two profiles are of different devices: /device:TPU:1 before, /device:TPU:113 now
where the time goes in v1:
time: 241 us
  Pallas kernels  232 us (96%)
  local copies, waits for them, and re-layouts  8.25 us (3%)
    pallas_call x1, Pallas kernels, per_device(): pl.pallas_call(return_kernel, out_shape=[jax.ShapeDtypeStruct((ROWS, HEAD...  118 us
    pallas_call x1, Pallas kernels, per_device(): pl.pallas_call(gather_kernel, out_shape=(jax.ShapeDtypeStruct((OWNED, CAP...  89.3 us
    pallas_call x1, Pallas kernels, per_device(): pl.pallas_call(attend_kernel, grid=(OWNED,), out_shape=jax.ShapeDtypeStru...  24.9 us
    unnamed x4, local copies, waits for them, and re-layouts  8.25 us

profile of v1, /device:TPU:113, one launch (start us, length us, event | category | flops | bytes accessed | tf_op | source)
XLA Modules:
  0.0 240.8 jit_solution(4265408703659115878)
XLA Ops:
  0.6 89.3 %gather.1 = (bf16[8,768,512]{2,1,0:T(8,128)(2,1)}, s32[8,1,384]{2,1,0:T(1,128)}) custom-call(bf16[384,1024]{1,0:T(8,128)(2,1)} %q_ref.1, bf16[384,1024]{1,0:T(8,128)(2,1)} %k_ref.1, bf16[384,1024]{1,0:T(8,128)(2,1)} %v_ref.1, bf16[384,1024]{1,0:T(8,128)(2,1)} %g_ref.1, s32[8,1,384]{2,1,0:T(1,128)} %bitcast.1, bf16[384,384]{1,0:T(8,128)(2,1)} %constant.2.clone.order_ref), custom_call_target="tpu_custom_call" | custom-call | tf_op jit(solution)/shard_map/gather/pallas_call | solution.py:312
  89.9 24.9 %attend.1.y_ref = bf16[8,768,512]{2,1,0:T(8,128)(2,1)} custom-call(bf16[8,768,512]{2,1,0:T(8,128)(2,1)} %get-tuple-element.6.x_ref), custom_call_target="tpu_custom_call" | custom-call | tf_op jit(solution)/shard_map/attend/pallas_call | solution.py:332
  114.8 117.7 %return.1 = (bf16[384,1024]{1,0:T(8,128)(2,1)}, bf16[384,1024]{1,0:T(8,128)(2,1)}, bf16[384,1024]{1,0:T(8,128)(2,1)}, bf16[384,1024]{1,0:T(8,128)(2,1)}) custom-call(bf16[8,768,512]{2,1,0:T(8,128)(2,1)} %attend.1.y_ref, s32[8,1,384]{2,1,0:T(1,128)} %get-tuple-element.7.slot_ref, bf16[384,384]{1,0:T(8,128)(2,1)} %constant.8.order_ref), custom_call_target="tpu_custom_call" | custom-call | tf_op jit(solution)/shard_map/return/pallas_call | solution.py:342
  232.6 2.1 copy.14
  234.6 2.1 copy.15
  236.7 2.1 copy.16
  238.7 2.1 copy.17

commit v2 on v0

v2 whole, which is shorter than its diff:
```python
import jax
import jax.numpy as jnp
import numpy as np
from jax import lax
from jax.experimental import pallas as pl
from jax.experimental.pallas import tpu as pltpu
from jax.sharding import PartitionSpec as P

MESH = pl.DeviceIdType.MESH
HEADS = 8
DIM = 128
ROWS = 384
CLUSTERS = 64
MOST = 12
LINE = 8
OWNED = 8
PIECE = OWNED * MOST
SLOTS = LINE * PIECE
CAP = LINE * LINE * MOST
HALF = SLOTS // 2
RUN = HALF // OWNED
WINDOW = 4
AHEAD = 2
ABSENT = 64.0
NEG = -1e30
SCALE = DIM ** -0.5
LOG2E = 1.4426950408889634
BLOCK_FWD = 384
BLOCK_BWD = 256
F32, BF16 = jnp.float32, jnp.bfloat16
NT = (((1,), (1,)), ((), ()))
VMEM = pltpu.VMEM
ANY = pl.ANY


def near(i):
    return jnp.where(i % 2 == 1, (i + 1) // 2, (LINE - i // 2) % LINE)


def far(i):
    return jnp.where(i % 2 == 1, 4 - (i + 1) // 2, 4 + i // 2)


def greet(z, r):
    barrier = pltpu.get_barrier_semaphore()
    for i in range(1, LINE):
        pl.semaphore_signal(
            barrier, inc=1, device_id={"seq": lax.rem(z + i, LINE) * LINE + r}, device_id_type=MESH
        )
        pl.semaphore_signal(
            barrier, inc=1, device_id={"seq": z * LINE + lax.rem(r + i, LINE)}, device_id_type=MESH
        )
    pl.semaphore_wait(barrier, 2 * (LINE - 1))


def wait_for(ref, sem):
    pltpu.make_async_copy(ref, ref, sem).wait()


def piece(o):
    return pl.ds(pl.multiple_of(o * PIECE, PIECE), PIECE)


def lanes(h):
    return pl.ds(pl.multiple_of(h * DIM, DIM), DIM)


def dot(a, b):
    return jnp.dot(a, b, preferred_element_type=F32)


def dot_nt(a, b):
    return lax.dot_general(a, b, NT, preferred_element_type=F32)


def mask(m):
    return m.astype(F32).astype(BF16)


def scores(k, q, bias, lo, hi):
    t = dot_nt(k[:hi], q) * (SCALE * LOG2E) + bias[:hi]
    late = (
        lax.broadcasted_iota(jnp.int32, (hi - lo, hi - lo), 0)
        > lax.broadcasted_iota(jnp.int32, (hi - lo, hi - lo), 1)
    )
    own = jnp.where(late, NEG, t[lo:hi])
    return jnp.concatenate([t[:lo], own], axis=0) if lo else own


def forward(x, o_ref, top_ref, inv_ref, j):
    k, vt = x[j, 1], x[j, 2].T
    bias = jnp.where(k[:, 0:1].astype(F32) > ABSENT / 2, NEG, 0.0)
    for lo in range(0, CAP, BLOCK_FWD):
        hi = lo + BLOCK_FWD
        t = scores(k, x[j, 0, lo:hi], bias, lo, hi)
        top = jnp.max(t, axis=0, keepdims=True)
        powered = jnp.exp2(t - top)
        inv = 1.0 / jnp.sum(powered, axis=0, keepdims=True)
        top_ref[j, :, lo:hi] = top
        inv_ref[j, :, lo:hi] = inv
        o_ref[j, lo:hi] = dot(vt[:, :hi], (powered * inv).astype(BF16)).T.astype(BF16)


def backward(x, o_ref, top_ref, inv_ref, dk_acc, dv_acc, j):
    k, v = x[j, 1], x[j, 2]
    kt = k.T
    bias = jnp.where(k[:, 0:1].astype(F32) > ABSENT / 2, NEG, 0.0)
    for lo in range(0, CAP, BLOCK_BWD):
        hi = lo + BLOCK_BWD
        q, g = x[j, 0, lo:hi], x[j, 3, lo:hi]
        t = scores(k, q, bias, lo, hi)
        weights = jnp.exp2(t - top_ref[j, :, lo:hi]) * inv_ref[j, :, lo:hi]
        dv = dot(weights.astype(BF16), g)
        row_dot = jnp.sum(
            (g.astype(F32) * o_ref[j, lo:hi].astype(F32)).T, axis=0, keepdims=True
        )
        ds = (weights * (dot_nt(v[:hi], g) - row_dot)).astype(BF16)
        dk = dot(ds, q)
        x[j, 0, lo:hi] = (dot(kt[:, :hi], ds) * SCALE).T.astype(BF16)
        if lo:
            dk_acc[:lo] += dk[:lo]
            dv_acc[:lo] += dv[:lo]
        dk_acc[lo:hi] = dk[lo:]
        dv_acc[lo:hi] = dv[lo:]
    x[j, 1] = (dk_acc[...] * SCALE).astype(BF16)
    x[j, 2] = dv_acc[...].astype(BF16)


def kernel(
    q_ref, k_ref, v_ref, g_ref, label_ref, order_ref, undo_ref,
    o_ref, dq_ref, dk_ref, dv_ref,
    zbuf, zlab, pick, back, xsrc, xbuf, ybuf, x, out, top, inv, dk_acc, dv_acc,
    z_send, z_recv, l_send, l_recv, x_send, x_recv, y_send, y_recv, o_send, o_recv,
):
    me = lax.axis_index("seq")
    z, r = me // LINE, me % LINE
    sources = (q_ref, k_ref, v_ref, g_ref)
    results = (o_ref, dq_ref, dk_ref, dv_ref)
    greet(z, r)

    def send_z(i, arrays):
        to = (z + near(i)) % LINE
        for a in arrays:
            pltpu.make_async_remote_copy(
                src_ref=sources[a].at[:, lanes(to)], dst_ref=zbuf.at[z, a],
                send_sem=z_send.at[i], recv_sem=z_recv.at[z, a],
                device_id={"seq": to * LINE + r}, device_id_type=MESH,
            ).start()

    def send_label(i, _):
        to = (z + near(i)) % LINE
        pltpu.make_async_remote_copy(
            src_ref=label_ref.at[to], dst_ref=zlab.at[z], send_sem=l_send, recv_sem=l_recv.at[z],
            device_id={"seq": to * LINE + r}, device_id_type=MESH,
        ).start()
        return 0

    def send_unit(u):
        @pl.when(u < LINE)
        def _():
            send_z(u, (0, 1, 2))

        @pl.when((u > LINE) & (u < 2 * LINE))
        def _():
            send_z(u - LINE, (3,))

    pltpu.make_async_copy(label_ref.at[z], zlab.at[z], l_recv.at[z]).start()
    for a in range(4):
        pltpu.make_async_copy(
            sources[a].at[:, lanes(z)], zbuf.at[z, a], z_recv.at[z, a]
        ).start()
    lax.fori_loop(1, LINE, send_label, 0)

    def first(u, _):
        send_z(u, (0, 1, 2))
        return 0

    lax.fori_loop(1, WINDOW, first, 0)

    before = mask(
        lax.broadcasted_iota(jnp.int32, (ROWS, ROWS), 0)
        < lax.broadcasted_iota(jnp.int32, (ROWS, ROWS), 1)
    )

    def to_owners(s, a, buf, send_sem, recv_sem):
        pltpu.make_async_copy(
            xsrc.at[s, a, piece(r)], buf.at[s, a, piece(r)], recv_sem.at[s, a]
        ).start()

        def send(n, _):
            o = (r + n) % LINE
            pltpu.make_async_remote_copy(
                src_ref=xsrc.at[s, a, piece(o)], dst_ref=buf.at[s, a, piece(r)],
                send_sem=send_sem.at[s, a], recv_sem=recv_sem.at[s, a],
                device_id={"seq": z * LINE + o}, device_id_type=MESH,
            ).start()
            return 0

        lax.fori_loop(1, LINE, send, 0)

    def pack(s, a, mark=None):
        wait_for(zbuf.at[s, a], z_recv.at[s, a])
        packed = dot(pick[s], zbuf[s, a])
        if mark is not None:
            packed = packed + mark
        xsrc[s, a] = packed.astype(BF16)
        to_owners(s, a, xbuf, x_send, x_recv)

    def regroup(i, arrays):
        s = (z - near(i) + LINE) % LINE
        for a in arrays:
            wait_for(xbuf.at[s, a], x_recv.at[s, a])
            for half in range(2):
                moved = dot(
                    order_ref[...], xbuf[s, a, half * HALF:(half + 1) * HALF]
                ).astype(BF16)
                for j in range(OWNED):
                    at = pl.multiple_of(s * PIECE + half * RUN, 16)
                    x[j, a, pl.ds(at, RUN), :] = moved[j * RUN:(j + 1) * RUN]

    def arrive(i, _):
        s = (z - near(i) + LINE) % LINE
        wait_for(zlab.at[s], l_recv.at[s])
        label = zlab[s]
        named = (
            lax.broadcasted_iota(jnp.int32, (CLUSTERS, ROWS), 0) == label
        ).astype(F32)
        rank = jnp.sum(named * dot(named.astype(BF16), before), axis=0, keepdims=True)
        slot = label * MOST + rank.astype(jnp.int32)
        chosen = (lax.broadcasted_iota(jnp.int32, (SLOTS, ROWS), 0) == slot).astype(F32)
        used = jnp.sum(chosen, axis=1, keepdims=True)
        mark = jnp.where(
            lax.broadcasted_iota(jnp.int32, (SLOTS, DIM), 1) == 0, (1.0 - used) * ABSENT, 0.0
        )
        pick[s] = chosen.astype(BF16)
        pack(s, 0)
        pack(s, 1, mark)
        pack(s, 2)
        send_unit(i + WINDOW)
        column = jnp.broadcast_to(slot.astype(F32), (DIM, ROWS)).T[:, 0:1].astype(jnp.int32)
        back[s] = mask(lax.broadcasted_iota(jnp.int32, (ROWS, SLOTS), 1) == column)

        @pl.when(i > 0)
        def _():
            regroup(i - 1, (0, 1, 2))

        return 0

    lax.fori_loop(0, LINE, arrive, 0)
    regroup(LINE - 1, (0, 1, 2))

    def arrive_g(i):
        pack((z - near(i) + LINE) % LINE, 3)
        send_unit(i + LINE + WINDOW)

        @pl.when(i > 0)
        def _():
            regroup(i - 1, (3,))

    def spread(i, a):
        s = (z + far(i)) % LINE
        wait_for(xsrc.at[s, a, pl.ds(0, SLOTS - PIECE)], x_send.at[s, a])
        for half in range(2):
            at = pl.multiple_of(s * PIECE + half * RUN, 16)
            taken = jnp.concatenate(
                [
                    out[j, pl.ds(at, RUN), :] if a == 0 else x[j, a - 1, pl.ds(at, RUN), :]
                    for j in range(OWNED)
                ],
                axis=0,
            )
            xsrc[s, a, half * HALF:(half + 1) * HALF] = dot(undo_ref[...], taken).astype(BF16)
        to_owners(s, a, ybuf, y_send, y_recv)

    def deliver(i, a):
        s = (z + far(i)) % LINE
        wait_for(ybuf.at[s, a], y_recv.at[s, a])
        zbuf[s, a] = dot(back[s], ybuf[s, a]).astype(BF16)

        @pl.when(i < LINE - 1)
        def _():
            pltpu.make_async_remote_copy(
                src_ref=zbuf.at[s, a], dst_ref=results[a].at[:, lanes(z)],
                send_sem=o_send.at[s], recv_sem=o_recv.at[z],
                device_id={"seq": s * LINE + r}, device_id_type=MESH,
            ).start()

        @pl.when(i == LINE - 1)
        def _():
            pltpu.make_async_copy(
                zbuf.at[z, a], results[a].at[:, lanes(z)], o_recv.at[z]
            ).start()

    def ahead(i, _):
        forward(x, out, top, inv, 2 * i)
        arrive_g(i)
        forward(x, out, top, inv, 2 * i + 1)
        return 0

    lax.fori_loop(0, 4, ahead, 0)

    def between(i, _):
        arrive_g(i + 4)
        spread(i, 0)
        return 0

    lax.fori_loop(0, 4, between, 0)
    regroup(LINE - 1, (3,))

    def behind(i, _):
        @pl.when(i < 4)
        def _():
            spread(i + 4, 0)

        deliver(i, 0)
        backward(x, out, top, inv, dk_acc, dv_acc, i)
        return 0

    lax.fori_loop(0, LINE, behind, 0)

    for i in range(AHEAD):
        for a in range(1, 4):
            spread(i, a)

    def leave(i, _):
        @pl.when(i + AHEAD < LINE)
        def _():
            for a in range(1, 4):
                spread(i + AHEAD, a)

        for a in range(1, 4):
            deliver(i, a)
        return 0

    lax.fori_loop(0, LINE, leave, 0)

    for a in range(4):
        def drain_y(i, _):
            wait_for(xsrc.at[i, a, pl.ds(0, SLOTS - PIECE)], y_send.at[i, a])
            return 0

        lax.fori_loop(0, LINE, drain_y, 0)

    def drain_z(i, _):
        wait_for(zbuf.at[i], o_recv.at[i])

        @pl.when(i != z)
        def _():
            wait_for(zbuf.at[i], o_send.at[i])

        @pl.when(i > 0)
        def _():
            wait_for(zbuf.at[i], z_send.at[i])
            wait_for(zlab.at[i], l_send)

        return 0

    lax.fori_loop(0, LINE, drain_z, 0)


def regroup_order():
    to = np.arange(HALF)
    source = (to % RUN) // MOST * PIECE + to // RUN * MOST + to % MOST
    return (to[None, :] == source[:, None]).astype(np.float32)


def per_device(queries, keys, values, grad_out, cluster):
    dma = pltpu.SemaphoreType.DMA
    labels = cluster.reshape(HEADS, 1, ROWS)
    order = regroup_order()
    return pl.pallas_call(
        kernel,
        out_shape=[jax.ShapeDtypeStruct((ROWS, HEADS * DIM), BF16)] * 4,
        in_specs=[pl.BlockSpec(memory_space=ANY)] * 4 + [pl.BlockSpec(memory_space=VMEM)] * 3,
        out_specs=[pl.BlockSpec(memory_space=ANY)] * 4,
        scratch_shapes=[
            VMEM((LINE, 4, ROWS, DIM), BF16),
            VMEM((LINE, 1, ROWS), jnp.int32),
            VMEM((LINE, SLOTS, ROWS), BF16),
            VMEM((LINE, ROWS, SLOTS), BF16),
            VMEM((LINE, 4, SLOTS, DIM), BF16),
            VMEM((LINE, 4, SLOTS, DIM), BF16),
            VMEM((LINE, 4, SLOTS, DIM), BF16),
            VMEM((OWNED, 4, CAP, DIM), BF16),
            VMEM((OWNED, CAP, DIM), BF16),
            VMEM((OWNED, 1, CAP), F32),
            VMEM((OWNED, 1, CAP), F32),
            VMEM((CAP, DIM), F32),
            VMEM((CAP, DIM), F32),
            dma((LINE,)), dma((LINE, 4)), dma, dma((LINE,)),
            dma((LINE, 4)), dma((LINE, 4)), dma((LINE, 4)), dma((LINE, 4)),
            dma((LINE,)), dma((LINE,)),
        ],
        compiler_params=pltpu.CompilerParams(
            collective_id=0, has_side_effects=True, vmem_limit_bytes=58 * 2**20
        ),
        name="attention",
    )(queries, keys, values, grad_out, labels, jnp.asarray(order, BF16), jnp.asarray(order.T, BF16))


def solution(mesh):
    return jax.shard_map(
        per_device,
        mesh=mesh,
        in_specs=(
            P(("grp", "seq"), None),
            P(("grp", "seq"), None),
            P(("grp", "seq"), None),
            P(("grp", "seq"), None),
            P(None, ("grp", "seq"), None),
        ),
        out_specs=(P(("grp", "seq"), None),) * 4,
        check_vma=False,
    )
```

time: 566 us -> 190 us (0.34); the launches traced: 555 us -> 190 us
  waiting for transfers between devices: 195 us -> 0 us
  Pallas kernels: 0 us -> 183 us
  local copies, waits for them, and re-layouts: 161 us -> 5.85 us
  matrix products: 97.1 us -> 0 us
  starting transfers between devices: 81.3 us -> 0 us
  other arithmetic: 18.8 us -> 0 us
    all_to_all x9 -> x0, waiting for transfers between devices: 195 us -> none  [the longest x1 36.9 us: per_device(): lax.all_to_all(back_slots(grad_query, seq_count), 'seq', split_axis=1, co...]
    pallas_call x0 -> x1, Pallas kernels: none -> 183 us  [per_device(): pl.pallas_call(kernel, out_shape=[jax.ShapeDtypeStruct((ROWS, HEADS * DIM...]
    dot_general x56 -> x0, matrix products: 97.1 us -> none  [the longest x16 25.1 us: probabilities(): jnp.einsum('cid,cjd->cij', query_slots, key_slots, preferred_element_type...]
    all_to_all x9 -> x0, starting transfers between devices: 81.3 us -> none  [the longest x1 18.5 us: per_device(): lax.all_to_all(value_buffer, 'seq', split_axis=0, concat_axis=0, tiled=True)]
    gather x4 -> x0, local copies, waits for them, and re-layouts: 78.9 us -> none  [unpack(): returned[head_ids, owners, inners]]
    unnamed x15 -> x10, local copies, waits for them, and re-layouts: 40.3 us -> 5.85 us
    while x9 -> x0, local copies, waits for them, and re-layouts: 20.5 us -> none  [the longest x4 12.7 us: gradients(): lax.map(gradients_one_head, (query_slots, key_slots, value_slots, valid_m...]
    reduce_sum x26 -> x0, other arithmetic: 16.6 us -> none  [the longest x8 8.83 us: gradients_one_head(): jnp.sum(grad_one.astype(jnp.float32) * output_one.astype(jnp.float32), ax...]
  transfers between devices with their start and end apart: 9 -> 0, of which waited for: 7 -> 0; matrix products, arithmetic and copies ran while one was open for 29% -> 0% of each run, Pallas kernels for 0% -> 0%
where the time goes in v2:
time: 190 us
  Pallas kernels  183 us (96%)
  local copies, waits for them, and re-layouts  5.85 us (3%)
    pallas_call x1, Pallas kernels, per_device(): pl.pallas_call(kernel, out_shape=[jax.ShapeDtypeStruct((ROWS, HEADS * DIM...  183 us
    unnamed x10, local copies, waits for them, and re-layouts  5.85 us

profile of v2, /device:TPU:1, one launch (start us, length us, event | category | flops | bytes accessed | tf_op | source)
XLA Modules:
  0.0 189.5 jit_solution(2896752552456025512)
XLA Ops:
  0.6 183.0 %attention.1 = (bf16[384,1024]{1,0:T(8,128)(2,1)}, bf16[384,1024]{1,0:T(8,128)(2,1)}, bf16[384,1024]{1,0:T(8,128)(2,1)}, bf16[384,1024]{1,0:T(8,128)(2,1)}) custom-call(bf16[384,1024]{1,0:T(8,128)(2,1)} %q_ref.1, bf16[384,1024]{1,0:T(8,128)(2,1)} %k_ref.1, bf16[384,1024]{1,0:T(8,128)(2,1)} %v_ref.1, bf16[384,1024]{1,0:T(8,128)(2,1)} %g_ref.1, ...), custom_call_target="tpu_custom_call" | custom-call | tf_op jit(solution)/shard_map/attention/pallas_call | solution.py:371
  183.7 0.0 copy-start.2
  183.7 2.1 %copy.15 = bf16[384,1024]{1,0:T(8,128)(2,1)} copy(bf16[384,1024]{1,0:T(8,128)(2,1)} %get-tuple-element.8) | data formatting | bytes 1572864
  185.8 0.0 copy-done.2
  185.8 0.0 copy-start.1
  185.8 0.9 copy.16
  186.7 0.5 copy-done.1
  187.2 0.0 copy-start
  187.2 0.9 copy.17
  188.1 0.5 copy-done
  188.6 0.9 copy.18
Async XLA Ops:
  183.7 2.1 %copy-start.2 = (bf16[384,1024]{1,0:T(8,128)(2,1)S(1)}, bf16[384,1024]{1,0:T(8,128)(2,1)}, u32[]{:S(2)}) copy-start(bf16[384,1024]{1,0:T(8,128)(2,1)} %get-tuple-element.9) | copy-start | bytes 2359300
  185.8 1.4 copy-start.1
  187.2 1.4 copy-start

commit v3 on v2

v3 whole, which is shorter than its diff:
```python
import jax
import jax.numpy as jnp
import numpy as np
from jax import lax
from jax.experimental import pallas as pl
from jax.experimental.pallas import tpu as pltpu
from jax.sharding import PartitionSpec as P

MESH = pl.DeviceIdType.MESH
HEADS = 8
DIM = 128
ROWS = 384
CLUSTERS = 64
MOST = 12
LINE = 8
OWNED = 8
PIECE = OWNED * MOST
SLOTS = LINE * PIECE
CAP = LINE * LINE * MOST
HALF = SLOTS // 2
RUN = HALF // OWNED
WINDOW = 6
AHEAD = 4
ABSENT = 64.0
NEG = -1e30
SCALE = DIM ** -0.5
LOG2E = 1.4426950408889634
BLOCK_FWD = 384
BLOCK_BWD = 256
F32, BF16 = jnp.float32, jnp.bfloat16
NT = (((1,), (1,)), ((), ()))
VMEM = pltpu.VMEM
ANY = pl.ANY


def inward(n):
    m = n - LINE // 2
    pair, late = m // 6 + 1, (n - 25) // 2 + 1
    dist = jnp.where(
        n < 4, 0,
        jnp.where(
            n < 22, jnp.where(m % 2 == 0, pair, LINE - pair),
            jnp.where(
                (n < 25) | (n == 31), 4, jnp.where(n % 2 == 1, late, LINE - late)
            ),
        ),
    )
    a = jnp.where(n < 4, n, jnp.where(n < 22, m % 6 // 2, jnp.where(n < 25, n - 22, 3)))
    return dist, a


def far(i):
    return jnp.where(i % 2 == 1, 4 - (i + 1) // 2, 4 + i // 2)


def outward(n):
    m = n - 3
    pair = 3 - m // 6
    dist = jnp.where(
        n < 3, 4, jnp.where(n < 21, jnp.where(m % 2 == 0, pair, LINE - pair), 0)
    )
    a = jnp.where(n < 3, n + 1, jnp.where(n < 21, m % 6 // 2 + 1, n - 20))
    return dist, a


def wait_for(ref, sem):
    pltpu.make_async_copy(ref, ref, sem).wait()


def piece(o):
    return pl.ds(pl.multiple_of(o * PIECE, PIECE), PIECE)


def lanes(h):
    return pl.ds(pl.multiple_of(h * DIM, DIM), DIM)


def dot(a, b):
    return jnp.dot(a, b, preferred_element_type=F32)


def dot_nt(a, b):
    return lax.dot_general(a, b, NT, preferred_element_type=F32)


def mask(m):
    return m.astype(F32).astype(BF16)


def scores(k, q, bias, lo, hi):
    t = dot_nt(k[:hi], q) * (SCALE * LOG2E) + bias[:hi]
    late = (
        lax.broadcasted_iota(jnp.int32, (hi - lo, hi - lo), 0)
        > lax.broadcasted_iota(jnp.int32, (hi - lo, hi - lo), 1)
    )
    own = jnp.where(late, NEG, t[lo:hi])
    return jnp.concatenate([t[:lo], own], axis=0) if lo else own


def forward(x, o_ref, top_ref, inv_ref, j):
    k, vt = x[j, 1], x[j, 2].T
    bias = jnp.where(k[:, 0:1].astype(F32) > ABSENT / 2, NEG, 0.0)
    for lo in range(0, CAP, BLOCK_FWD):
        hi = lo + BLOCK_FWD
        t = scores(k, x[j, 0, lo:hi], bias, lo, hi)
        top = jnp.max(t, axis=0, keepdims=True)
        powered = jnp.exp2(t - top)
        inv = 1.0 / jnp.sum(powered, axis=0, keepdims=True)
        top_ref[j, :, lo:hi] = top
        inv_ref[j, :, lo:hi] = inv
        o_ref[j, lo:hi] = dot(vt[:, :hi], (powered * inv).astype(BF16)).T.astype(BF16)


def backward(x, o_ref, top_ref, inv_ref, dk_acc, dv_acc, j):
    k, v = x[j, 1], x[j, 2]
    kt = k.T
    bias = jnp.where(k[:, 0:1].astype(F32) > ABSENT / 2, NEG, 0.0)
    for lo in range(0, CAP, BLOCK_BWD):
        hi = lo + BLOCK_BWD
        q, g = x[j, 0, lo:hi], x[j, 3, lo:hi]
        t = scores(k, q, bias, lo, hi)
        weights = jnp.exp2(t - top_ref[j, :, lo:hi]) * inv_ref[j, :, lo:hi]
        dv = dot(weights.astype(BF16), g)
        row_dot = jnp.sum(
            (g.astype(F32) * o_ref[j, lo:hi].astype(F32)).T, axis=0, keepdims=True
        )
        ds = (weights * (dot_nt(v[:hi], g) - row_dot)).astype(BF16)
        dk = dot(ds, q)
        x[j, 0, lo:hi] = (dot(kt[:, :hi], ds) * SCALE).T.astype(BF16)
        if lo:
            dk_acc[:lo] += dk[:lo]
            dv_acc[:lo] += dv[:lo]
        dk_acc[lo:hi] = dk[lo:]
        dv_acc[lo:hi] = dv[lo:]
    x[j, 1] = (dk_acc[...] * SCALE).astype(BF16)
    x[j, 2] = dv_acc[...].astype(BF16)


def kernel(
    q_ref, k_ref, v_ref, g_ref, label_ref, order_ref, undo_ref,
    o_ref, dq_ref, dk_ref, dv_ref,
    zbuf, zlab, pick, back, xsrc, xbuf, ybuf, x, out, top, inv, dk_acc, dv_acc,
    z_send, z_recv, l_send, l_recv, x_send, x_recv, y_send, y_recv, o_send, o_recv,
):
    me = lax.axis_index("seq")
    z, r = me // LINE, me % LINE
    sources = (q_ref, k_ref, v_ref, g_ref)
    results = (o_ref, dq_ref, dk_ref, dv_ref)

    barrier = pltpu.get_barrier_semaphore()
    for i in range(1, LINE):
        pl.semaphore_signal(
            barrier, inc=1, device_id={"seq": lax.rem(z + i, LINE) * LINE + r}, device_id_type=MESH
        )
        pl.semaphore_signal(
            barrier, inc=1, device_id={"seq": z * LINE + lax.rem(r + i, LINE)}, device_id_type=MESH
        )

    pltpu.make_async_copy(label_ref.at[z], zlab.at[z], l_recv.at[z]).start()
    for a in range(4):
        pltpu.make_async_copy(
            sources[a].at[:, lanes(z)], zbuf.at[z, a], z_recv.at[z, a]
        ).start()

    before = mask(
        lax.broadcasted_iota(jnp.int32, (ROWS, ROWS), 0)
        < lax.broadcasted_iota(jnp.int32, (ROWS, ROWS), 1)
    )

    def prepare(s):
        wait_for(zlab.at[s], l_recv.at[s])
        label = zlab[s]
        named = (
            lax.broadcasted_iota(jnp.int32, (CLUSTERS, ROWS), 0) == label
        ).astype(F32)
        rank = jnp.sum(named * dot(named.astype(BF16), before), axis=0, keepdims=True)
        slot = label * MOST + rank.astype(jnp.int32)
        pick[s] = mask(lax.broadcasted_iota(jnp.int32, (SLOTS, ROWS), 0) == slot)
        column = jnp.broadcast_to(slot.astype(F32), (DIM, ROWS)).T[:, 0:1].astype(jnp.int32)
        back[s] = mask(lax.broadcasted_iota(jnp.int32, (ROWS, SLOTS), 1) == column)

    prepare(z)
    pl.semaphore_wait(barrier, 2 * (LINE - 1))

    def send_z(n, _):
        dist, at = inward(n)
        to = (z + dist) % LINE
        for a in range(4):
            @pl.when(at == a)
            def _():
                pltpu.make_async_remote_copy(
                    src_ref=sources[a].at[:, lanes(to)], dst_ref=zbuf.at[z, a],
                    send_sem=z_send.at[dist], recv_sem=z_recv.at[z, a],
                    device_id={"seq": to * LINE + r}, device_id_type=MESH,
                ).start()
        return 0

    def send_label(i, _):
        to = (z + i) % LINE
        pltpu.make_async_remote_copy(
            src_ref=label_ref.at[to], dst_ref=zlab.at[z], send_sem=l_send, recv_sem=l_recv.at[z],
            device_id={"seq": to * LINE + r}, device_id_type=MESH,
        ).start()
        return 0

    lax.fori_loop(1, LINE, send_label, 0)
    lax.fori_loop(4, 4 + WINDOW, send_z, 0)

    def to_owners(s, a, buf, send_sem, recv_sem):
        pltpu.make_async_copy(
            xsrc.at[s, a, piece(r)], buf.at[s, a, piece(r)], recv_sem.at[s, a]
        ).start()

        def send(n, _):
            o = (r + n) % LINE
            pltpu.make_async_remote_copy(
                src_ref=xsrc.at[s, a, piece(o)], dst_ref=buf.at[s, a, piece(r)],
                send_sem=send_sem.at[s, a], recv_sem=recv_sem.at[s, a],
                device_id={"seq": z * LINE + o}, device_id_type=MESH,
            ).start()
            return 0

        lax.fori_loop(1, LINE, send, 0)

    def pack(n, _):
        dist, a = inward(n)
        s = (z - dist + LINE) % LINE

        @pl.when((a == 0) & (n > 0))
        def _():
            prepare(s)

        wait_for(zbuf.at[s, a], z_recv.at[s, a])
        xsrc[s, a] = dot(pick[s], zbuf[s, a]).astype(BF16)

        @pl.when(a == 1)
        def _():
            used = jnp.sum(pick[s].astype(F32), axis=1, keepdims=True)
            first = lax.broadcasted_iota(jnp.int32, (SLOTS, DIM), 1) == 0
            mark = jnp.where(first, (1.0 - used) * ABSENT, 0.0)
            xsrc[s, 1] = (xsrc[s, 1].astype(F32) + mark).astype(BF16)

        to_owners(s, a, xbuf, x_send, x_recv)

        @pl.when((n + WINDOW >= 4 + WINDOW) & (n + WINDOW < 32))
        def _():
            send_z(n + WINDOW, 0)

        return 0

    def regroup(n, _):
        dist, a = inward(n)
        s = (z - dist + LINE) % LINE
        wait_for(xbuf.at[s, a], x_recv.at[s, a])
        for half in range(2):
            moved = dot(
                order_ref[...], xbuf[s, a, half * HALF:(half + 1) * HALF]
            ).astype(BF16)
            for j in range(OWNED):
                at = pl.multiple_of(s * PIECE + half * RUN, 16)
                x[j, a, pl.ds(at, RUN), :] = moved[j * RUN:(j + 1) * RUN]
        return 0

    def arrive(n, _):
        pack(n, 0)
        lo = jnp.where(n < 16, jnp.maximum(n - 7, 0), 9 + (3 * (n - 16) + 1) // 2)
        hi = jnp.where(n < 16, jnp.maximum(n - 6, 0), lo + 2 - n % 2)
        lax.fori_loop(lo, hi, regroup, 0)
        return 0

    def spread(s, a, taken):
        wait_for(xsrc.at[s, a, pl.ds(0, SLOTS - PIECE)], x_send.at[s, a])
        for half in range(2):
            at = pl.multiple_of(s * PIECE + half * RUN, 16)
            rows = jnp.concatenate([taken(j, pl.ds(at, RUN)) for j in range(OWNED)], axis=0)
            xsrc[s, a, half * HALF:(half + 1) * HALF] = dot(undo_ref[...], rows).astype(BF16)
        to_owners(s, a, ybuf, y_send, y_recv)

    def spread_out(i, _):
        spread((z + far(i)) % LINE, 0, lambda j, rows: out[j, rows, :])
        return 0

    def spread_grad(n, _):
        dist, a = outward(n)
        spread((z + dist) % LINE, a, lambda j, rows: x[j, a - 1, rows, :])
        return 0

    def deliver(s, at, arrays):
        wait_for(ybuf.at[s, at], y_recv.at[s, at])
        zbuf[s, at] = dot(back[s], ybuf[s, at]).astype(BF16)
        for a in arrays:
            @pl.when((at == a) & (s != z))
            def _():
                pltpu.make_async_remote_copy(
                    src_ref=zbuf.at[s, a], dst_ref=results[a].at[:, lanes(z)],
                    send_sem=o_send.at[s], recv_sem=o_recv.at[z],
                    device_id={"seq": s * LINE + r}, device_id_type=MESH,
                ).start()

            @pl.when((at == a) & (s == z))
            def _():
                pltpu.make_async_copy(
                    zbuf.at[z, a], results[a].at[:, lanes(z)], o_recv.at[z]
                ).start()

    lax.fori_loop(0, 25, arrive, 0)
    lax.fori_loop(25, 27, pack, 0)
    lax.fori_loop(23, 25, regroup, 0)

    def ahead(i, _):
        forward(x, out, top, inv, 2 * i)
        forward(x, out, top, inv, 2 * i + 1)
        lo = jnp.where(i == 0, 27, jnp.where(i < 3, 29, 31))
        hi = jnp.where(i < 2, 29, jnp.where(i == 2, 31, 32))
        lax.fori_loop(lo, hi, pack, 0)
        lo = jnp.where(i < 2, 25, 27)
        hi = jnp.where(i == 0, 25, jnp.where(i < 3, 27, 29))
        lax.fori_loop(lo, hi, regroup, 0)
        return 0

    lax.fori_loop(0, 4, ahead, 0)
    lax.fori_loop(0, 3, spread_out, 0)
    lax.fori_loop(29, 32, regroup, 0)

    def behind(i, _):
        backward(x, out, top, inv, dk_acc, dv_acc, i)
        deliver((z + far(i)) % LINE, 0, (0,))

        @pl.when(i + 3 < LINE)
        def _():
            spread_out(i + 3, 0)

        return 0

    lax.fori_loop(0, LINE, behind, 0)
    lax.fori_loop(0, AHEAD, spread_grad, 0)

    def leave(n, _):
        @pl.when(n + AHEAD < 24)
        def _():
            spread_grad(n + AHEAD, 0)

        dist, a = outward(n)
        deliver((z + dist) % LINE, a, (1, 2, 3))
        return 0

    lax.fori_loop(0, 24, leave, 0)

    def drain(i, _):
        wait_for(zbuf.at[i], o_recv.at[i])
        for a in range(4):
            wait_for(xsrc.at[i, a, pl.ds(0, SLOTS - PIECE)], y_send.at[i, a])

        @pl.when(i != z)
        def _():
            wait_for(zbuf.at[i], o_send.at[i])

        @pl.when(i > 0)
        def _():
            wait_for(zbuf.at[i], z_send.at[i])
            wait_for(zlab.at[i], l_send)

        return 0

    lax.fori_loop(0, LINE, drain, 0)


def regroup_order():
    to = np.arange(HALF)
    source = (to % RUN) // MOST * PIECE + to // RUN * MOST + to % MOST
    return (to[None, :] == source[:, None]).astype(np.float32)


def per_device(queries, keys, values, grad_out, cluster):
    dma = pltpu.SemaphoreType.DMA
    labels = cluster.reshape(HEADS, 1, ROWS)
    order = regroup_order()
    return pl.pallas_call(
        kernel,
        out_shape=[jax.ShapeDtypeStruct((ROWS, HEADS * DIM), BF16)] * 4,
        in_specs=[pl.BlockSpec(memory_space=ANY)] * 4 + [pl.BlockSpec(memory_space=VMEM)] * 3,
        out_specs=[pl.BlockSpec(memory_space=ANY)] * 4,
        scratch_shapes=[
            VMEM((LINE, 4, ROWS, DIM), BF16),
            VMEM((LINE, 1, ROWS), jnp.int32),
            VMEM((LINE, SLOTS, ROWS), BF16),
            VMEM((LINE, ROWS, SLOTS), BF16),
            VMEM((LINE, 4, SLOTS, DIM), BF16),
            VMEM((LINE, 4, SLOTS, DIM), BF16),
            VMEM((LINE, 4, SLOTS, DIM), BF16),
            VMEM((OWNED, 4, CAP, DIM), BF16),
            VMEM((OWNED, CAP, DIM), BF16),
            VMEM((OWNED, 1, CAP), F32),
            VMEM((OWNED, 1, CAP), F32),
            VMEM((CAP, DIM), F32),
            VMEM((CAP, DIM), F32),
            dma((LINE,)), dma((LINE, 4)), dma, dma((LINE,)),
            dma((LINE, 4)), dma((LINE, 4)), dma((LINE, 4)), dma((LINE, 4)),
            dma((LINE,)), dma((LINE,)),
        ],
        compiler_params=pltpu.CompilerParams(
            collective_id=0, has_side_effects=True, vmem_limit_bytes=58 * 2**20
        ),
        name="attention",
    )(queries, keys, values, grad_out, labels, jnp.asarray(order, BF16), jnp.asarray(order.T, BF16))


def solution(mesh):
    return jax.shard_map(
        per_device,
        mesh=mesh,
        in_specs=(
            P(("grp", "seq"), None),
            P(("grp", "seq"), None),
            P(("grp", "seq"), None),
            P(("grp", "seq"), None),
            P(None, ("grp", "seq"), None),
        ),
        out_specs=(P(("grp", "seq"), None),) * 4,
        check_vma=False,
    )
```

time: 190 us -> 178 us (0.937)
  Pallas kernels: 183 us -> 171 us
    pallas_call x1, Pallas kernels: 183 us -> 171 us  [per_device(): pl.pallas_call(kernel, out_shape=[jax.ShapeDtypeStruct((ROWS, HEADS * DIM...]
where the time goes in v3:
time: 178 us; the launch traced here: 177 us
  Pallas kernels  171 us (96%)
  local copies, waits for them, and re-layouts  5.85 us (3%)
    pallas_call x1, Pallas kernels, per_device(): pl.pallas_call(kernel, out_shape=[jax.ShapeDtypeStruct((ROWS, HEADS * DIM...  171 us
    unnamed x10, local copies, waits for them, and re-layouts  5.85 us

profile of v3, /device:TPU:1, one launch (start us, length us, event | category | flops | bytes accessed | tf_op | source)
XLA Modules:
  0.0 177.3 jit_solution(5181356060925780412)
XLA Ops:
  0.6 170.8 %attention.1 = (bf16[384,1024]{1,0:T(8,128)(2,1)}, bf16[384,1024]{1,0:T(8,128)(2,1)}, bf16[384,1024]{1,0:T(8,128)(2,1)}, bf16[384,1024]{1,0:T(8,128)(2,1)}) custom-call(bf16[384,1024]{1,0:T(8,128)(2,1)} %q_ref.1, bf16[384,1024]{1,0:T(8,128)(2,1)} %k_ref.1, bf16[384,1024]{1,0:T(8,128)(2,1)} %v_ref.1, bf16[384,1024]{1,0:T(8,128)(2,1)} %g_ref.1, ...), custom_call_target="tpu_custom_call" | custom-call | tf_op jit(solution)/shard_map/attention/pallas_call | solution.py:378
  171.5 0.0 copy-start.2
  171.5 2.1 %copy.15 = bf16[384,1024]{1,0:T(8,128)(2,1)} copy(bf16[384,1024]{1,0:T(8,128)(2,1)} %get-tuple-element.8) | data formatting | bytes 1572864
  173.6 0.0 copy-done.2
  173.6 0.0 copy-start.1
  173.6 0.9 copy.16
  174.5 0.5 copy-done.1
  175.1 0.0 copy-start
  175.1 0.9 copy.17
  175.9 0.5 copy-done
  176.5 0.9 copy.18
Async XLA Ops:
  171.5 2.1 %copy-start.2 = (bf16[384,1024]{1,0:T(8,128)(2,1)S(1)}, bf16[384,1024]{1,0:T(8,128)(2,1)}, u32[]{:S(2)}) copy-start(bf16[384,1024]{1,0:T(8,128)(2,1)} %get-tuple-element.9) | copy-start | bytes 2359300
  173.6 1.4 copy-start.1
  175.1 1.4 copy-start

commit v4 on v3

--- a/solution.py
+++ b/solution.py
@@ -20,7 +20,8 @@
 HALF = SLOTS // 2
 RUN = HALF // OWNED
 WINDOW = 6
-AHEAD = 4
+AHEAD = 6
+PARTS = 3
 ABSENT = 64.0
 NEG = -1e30
 SCALE = DIM ** -0.5
@@ -34,32 +35,33 @@
 
 
 def inward(n):
-    m = n - LINE // 2
-    pair, late = m // 6 + 1, (n - 25) // 2 + 1
+    m = n - 4
+    pair, late = m // 4 + 1, (n - 18) % 7
+    signed = jnp.where(m % 2 == 0, pair, LINE - pair)
+    alone = jnp.where(
+        late == 6, 4, jnp.where(late % 2 == 0, late // 2 + 1, LINE - 1 - late // 2)
+    )
     dist = jnp.where(
-        n < 4, 0,
-        jnp.where(
-            n < 22, jnp.where(m % 2 == 0, pair, LINE - pair),
-            jnp.where(
-                (n < 25) | (n == 31), 4, jnp.where(n % 2 == 1, late, LINE - late)
-            ),
-        ),
-    )
-    a = jnp.where(n < 4, n, jnp.where(n < 22, m % 6 // 2, jnp.where(n < 25, n - 22, 3)))
+        n < 4, 0, jnp.where(n < 16, signed, jnp.where(n < 18, 4, alone))
+    )
+    a = jnp.where(
+        n < 4, n, jnp.where(n < 16, m % 4 // 2, jnp.where(n < 18, n - 16, jnp.where(n < 25, 2, 3)))
+    )
     return dist, a
 
 
-def far(i):
-    return jnp.where(i % 2 == 1, 4 - (i + 1) // 2, 4 + i // 2)
-
-
 def outward(n):
-    m = n - 3
-    pair = 3 - m // 6
+    i, m = n % LINE, n - 18
+    pair = 3 - m // 4
+    alone = jnp.where(i % 2 == 1, 4 - (i + 1) // 2, 4 + i // 2)
+    signed = jnp.where(m % 2 == 0, pair, LINE - pair)
     dist = jnp.where(
-        n < 3, 4, jnp.where(n < 21, jnp.where(m % 2 == 0, pair, LINE - pair), 0)
-    )
-    a = jnp.where(n < 3, n + 1, jnp.where(n < 21, m % 6 // 2 + 1, n - 20))
+        n < 16, alone, jnp.where(n < 18, 4, jnp.where(n < 30, signed, 0))
+    )
+    a = jnp.where(
+        n < 8, 0,
+        jnp.where(n < 16, 3, jnp.where(n < 18, n - 15, jnp.where(n < 30, m % 4 // 2 + 1, n - 29))),
+    )
     return dist, a
 
 
@@ -97,9 +99,10 @@
     return jnp.concatenate([t[:lo], own], axis=0) if lo else own
 
 
-def forward(x, o_ref, top_ref, inv_ref, j):
-    k, vt = x[j, 1], x[j, 2].T
+def softmax(x, weights, top_ref, inv_ref, j):
+    k = x[j, 1]
     bias = jnp.where(k[:, 0:1].astype(F32) > ABSENT / 2, NEG, 0.0)
+    at = 0
     for lo in range(0, CAP, BLOCK_FWD):
         hi = lo + BLOCK_FWD
         t = scores(k, x[j, 0, lo:hi], bias, lo, hi)
@@ -108,10 +111,28 @@
         inv = 1.0 / jnp.sum(powered, axis=0, keepdims=True)
         top_ref[j, :, lo:hi] = top
         inv_ref[j, :, lo:hi] = inv
-        o_ref[j, lo:hi] = dot(vt[:, :hi], (powered * inv).astype(BF16)).T.astype(BF16)
-
-
-def backward(x, o_ref, top_ref, inv_ref, dk_acc, dv_acc, j):
+        weights[j, at:at + hi] = (powered * inv).astype(BF16)
+        at += hi
+
+
+def attend(x, y, weights, j):
+    vt = x[j, 2].T
+    at = 0
+    for hi in range(BLOCK_FWD, CAP + 1, BLOCK_FWD):
+        y[j, 0, hi - BLOCK_FWD:hi] = dot(vt[:, :hi], weights[j, at:at + hi]).T.astype(BF16)
+        at += hi
+
+
+def value_gradient(x, y, weights, j):
+    g = x[j, 3]
+    half = BLOCK_FWD
+    y[j, 3, :half] = (
+        dot(weights[j, :half], g[:half]) + dot(weights[j, half:2 * half], g[half:])
+    ).astype(BF16)
+    y[j, 3, half:] = dot(weights[j, 2 * half:], g[half:]).astype(BF16)
+
+
+def backward(x, y, top_ref, inv_ref, dk_acc, j):
     k, v = x[j, 1], x[j, 2]
     kt = k.T
     bias = jnp.where(k[:, 0:1].astype(F32) > ABSENT / 2, NEG, 0.0)
@@ -120,26 +141,22 @@
         q, g = x[j, 0, lo:hi], x[j, 3, lo:hi]
         t = scores(k, q, bias, lo, hi)
         weights = jnp.exp2(t - top_ref[j, :, lo:hi]) * inv_ref[j, :, lo:hi]
-        dv = dot(weights.astype(BF16), g)
         row_dot = jnp.sum(
-            (g.astype(F32) * o_ref[j, lo:hi].astype(F32)).T, axis=0, keepdims=True
+            (g.astype(F32) * y[j, 0, lo:hi].astype(F32)).T, axis=0, keepdims=True
         )
         ds = (weights * (dot_nt(v[:hi], g) - row_dot)).astype(BF16)
         dk = dot(ds, q)
-        x[j, 0, lo:hi] = (dot(kt[:, :hi], ds) * SCALE).T.astype(BF16)
+        y[j, 1, lo:hi] = (dot(kt[:, :hi], ds) * SCALE).T.astype(BF16)
         if lo:
             dk_acc[:lo] += dk[:lo]
-            dv_acc[:lo] += dv[:lo]
         dk_acc[lo:hi] = dk[lo:]
-        dv_acc[lo:hi] = dv[lo:]
-    x[j, 1] = (dk_acc[...] * SCALE).astype(BF16)
-    x[j, 2] = dv_acc[...].astype(BF16)
+    y[j, 2] = (dk_acc[...] * SCALE).astype(BF16)
 
 
 def kernel(
     q_ref, k_ref, v_ref, g_ref, label_ref, order_ref, undo_ref,
     o_ref, dq_ref, dk_ref, dv_ref,
-    zbuf, zlab, pick, back, xsrc, xbuf, ybuf, x, out, top, inv, dk_acc, dv_acc,
+    zbuf, zlab, pick, back, xsrc, xbuf, ybuf, x, y, weights, top, inv, dk_acc,
     z_send, z_recv, l_send, l_recv, x_send, x_recv, y_send, y_recv, o_send, o_recv,
 ):
     me = lax.axis_index("seq")
@@ -263,32 +280,28 @@
 
     def arrive(n, _):
         pack(n, 0)
-        lo = jnp.where(n < 16, jnp.maximum(n - 7, 0), 9 + (3 * (n - 16) + 1) // 2)
-        hi = jnp.where(n < 16, jnp.maximum(n - 6, 0), lo + 2 - n % 2)
+        lo = jnp.where(n < 14, jnp.maximum(n - 7, 0), 7 + (3 * (n - 14) + 1) // 2)
+        hi = jnp.where(n < 14, jnp.maximum(n - 6, 0), lo + 2 - n % 2)
         lax.fori_loop(lo, hi, regroup, 0)
         return 0
 
-    def spread(s, a, taken):
+    def spread(n, _):
+        dist, a = outward(n)
+        s = (z + dist) % LINE
         wait_for(xsrc.at[s, a, pl.ds(0, SLOTS - PIECE)], x_send.at[s, a])
         for half in range(2):
             at = pl.multiple_of(s * PIECE + half * RUN, 16)
-            rows = jnp.concatenate([taken(j, pl.ds(at, RUN)) for j in range(OWNED)], axis=0)
+            rows = jnp.concatenate([y[j, a, pl.ds(at, RUN), :] for j in range(OWNED)], axis=0)
             xsrc[s, a, half * HALF:(half + 1) * HALF] = dot(undo_ref[...], rows).astype(BF16)
         to_owners(s, a, ybuf, y_send, y_recv)
-
-    def spread_out(i, _):
-        spread((z + far(i)) % LINE, 0, lambda j, rows: out[j, rows, :])
-        return 0
-
-    def spread_grad(n, _):
-        dist, a = outward(n)
-        spread((z + dist) % LINE, a, lambda j, rows: x[j, a - 1, rows, :])
-        return 0
-
-    def deliver(s, at, arrays):
+        return 0
+
+    def deliver(n, _):
+        dist, at = outward(n)
+        s = (z + dist) % LINE
         wait_for(ybuf.at[s, at], y_recv.at[s, at])
         zbuf[s, at] = dot(back[s], ybuf[s, at]).astype(BF16)
-        for a in arrays:
+        for a in range(4):
             @pl.when((at == a) & (s != z))
             def _():
                 pltpu.make_async_remote_copy(
@@ -302,49 +315,80 @@
                 pltpu.make_async_copy(
                     zbuf.at[z, a], results[a].at[:, lanes(z)], o_recv.at[z]
                 ).start()
-
-    lax.fori_loop(0, 25, arrive, 0)
+        return 0
+
+    lax.fori_loop(0, 18, arrive, 0)
+    lax.fori_loop(18, 20, pack, 0)
+    lax.fori_loop(13, 18, regroup, 0)
+    lax.fori_loop(20, 22, pack, 0)
+
+    def score(i, _):
+        softmax(x, weights, top, inv, 2 * i)
+        softmax(x, weights, top, inv, 2 * i + 1)
+        lo = jnp.where(i < 3, 22, 24)
+        hi = jnp.where(i < 2, 22, jnp.where(i < 3, 24, 25))
+        lax.fori_loop(lo, hi, pack, 0)
+        regroup(18 + i, 0)
+        return 0
+
+    lax.fori_loop(0, 4, score, 0)
     lax.fori_loop(25, 27, pack, 0)
-    lax.fori_loop(23, 25, regroup, 0)
-
-    def ahead(i, _):
-        forward(x, out, top, inv, 2 * i)
-        forward(x, out, top, inv, 2 * i + 1)
-        lo = jnp.where(i == 0, 27, jnp.where(i < 3, 29, 31))
-        hi = jnp.where(i < 2, 29, jnp.where(i == 2, 31, 32))
-        lax.fori_loop(lo, hi, pack, 0)
-        lo = jnp.where(i < 2, 25, 27)
-        hi = jnp.where(i == 0, 25, jnp.where(i < 3, 27, 29))
-        lax.fori_loop(lo, hi, regroup, 0)
-        return 0
-
-    lax.fori_loop(0, 4, ahead, 0)
-    lax.fori_loop(0, 3, spread_out, 0)
-    lax.fori_loop(29, 32, regroup, 0)
+    lax.fori_loop(22, 25, regroup, 0)
+
+    def attend_one(j, _):
+        attend(x, y, weights, j)
+        return 0
+
+    lax.fori_loop(0, OWNED, attend_one, 0)
+    lax.fori_loop(0, 3, spread, 0)
+    lax.fori_loop(27, 29, pack, 0)
+    deliver(0, 0)
+    lax.fori_loop(25, 27, regroup, 0)
+    deliver(1, 0)
+    lax.fori_loop(29, 31, pack, 0)
+    deliver(2, 0)
+    pack(31, 0)
+    lax.fori_loop(3, 5, spread, 0)
+    lax.fori_loop(27, 32, regroup, 0)
+
+    def value_one(j, _):
+        value_gradient(x, y, weights, j)
+
+        @pl.when(j < 3)
+        def _():
+            spread(j + 5, 0)
+
+        @pl.when(j % 4 == 3)
+        def _():
+            deliver(3 + j // 4, 0)
+
+        return 0
+
+    lax.fori_loop(0, OWNED, value_one, 0)
+    lax.fori_loop(8, 10, spread, 0)
 
     def behind(i, _):
-        backward(x, out, top, inv, dk_acc, dv_acc, i)
-        deliver((z + far(i)) % LINE, 0, (0,))
-
-        @pl.when(i + 3 < LINE)
-        def _():
-            spread_out(i + 3, 0)
-
-        return 0
-
-    lax.fori_loop(0, LINE, behind, 0)
-    lax.fori_loop(0, AHEAD, spread_grad, 0)
+        backward(x, y, top, inv, dk_acc, i)
+        deliver(i + 5, 0)
+
+        @pl.when(i < 6)
+        def _():
+            spread(i + 10, 0)
+
+        return 0
+
+    lax.fori_loop(0, OWNED, behind, 0)
+    lax.fori_loop(16, 13 + AHEAD, spread, 0)
 
     def leave(n, _):
-        @pl.when(n + AHEAD < 24)
-        def _():
-            spread_grad(n + AHEAD, 0)
-
-        dist, a = outward(n)
-        deliver((z + dist) % LINE, a, (1, 2, 3))
-        return 0
-
-    lax.fori_loop(0, 24, leave, 0)
+        @pl.when(n + AHEAD < 32)
+        def _():
+            spread(n + AHEAD, 0)
+
+        deliver(n, 0)
+        return 0
+
+    lax.fori_loop(13, 32, leave, 0)
 
     def drain(i, _):
         wait_for(zbuf.at[i], o_recv.at[i])
@@ -371,11 +415,16 @@
     return (to[None, :] == source[:, None]).astype(np.float32)
 
 
+def finish_kernel(*refs):
+    for a in range(4):
+        refs[4 + a][...] = refs[a][...]
+
+
 def per_device(queries, keys, values, grad_out, cluster):
     dma = pltpu.SemaphoreType.DMA
     labels = cluster.reshape(HEADS, 1, ROWS)
     order = regroup_order()
-    return pl.pallas_call(
+    outs = pl.pallas_call(
         kernel,
         out_shape=[jax.ShapeDtypeStruct((ROWS, HEADS * DIM), BF16)] * 4,
         in_specs=[pl.BlockSpec(memory_space=ANY)] * 4 + [pl.BlockSpec(memory_space=VMEM)] * 3,
@@ -389,20 +438,29 @@
             VMEM((LINE, 4, SLOTS, DIM), BF16),
             VMEM((LINE, 4, SLOTS, DIM), BF16),
             VMEM((OWNED, 4, CAP, DIM), BF16),
-            VMEM((OWNED, CAP, DIM), BF16),
+            VMEM((OWNED, 4, CAP, DIM), BF16),
+            VMEM((OWNED, 3 * BLOCK_FWD, BLOCK_FWD), BF16),
             VMEM((OWNED, 1, CAP), F32),
             VMEM((OWNED, 1, CAP), F32),
-            VMEM((CAP, DIM), F32),
             VMEM((CAP, DIM), F32),
             dma((LINE,)), dma((LINE, 4)), dma, dma((LINE,)),
             dma((LINE, 4)), dma((LINE, 4)), dma((LINE, 4)), dma((LINE, 4)),
             dma((LINE,)), dma((LINE,)),
         ],
         compiler_params=pltpu.CompilerParams(
-            collective_id=0, has_side_effects=True, vmem_limit_bytes=58 * 2**20
+            collective_id=0, has_side_effects=True, vmem_limit_bytes=60 * 2**20
         ),
         name="attention",
     )(queries, keys, values, grad_out, labels, jnp.asarray(order, BF16), jnp.asarray(order.T, BF16))
+    spec = pl.BlockSpec((ROWS // PARTS, HEADS * DIM), lambda i: (i, 0))
+    return pl.pallas_call(
+        finish_kernel,
+        grid=(PARTS,),
+        out_shape=[jax.ShapeDtypeStruct((ROWS, HEADS * DIM), BF16)] * 4,
+        in_specs=[spec] * 4,
+        out_specs=[spec] * 4,
+        name="finish",
+    )(*outs)
 
 
 def solution(mesh):

time: 178 us -> 173 us (0.972)
  local copies, waits for them, and re-layouts: 5.85 us -> 0 us
    unnamed x10 -> x0, local copies, waits for them, and re-layouts: 5.85 us -> none
    pallas_call x0 -> x1, Pallas kernels: none -> 4.32 us  [per_device(): pl.pallas_call(finish_kernel, grid=(PARTS,), out_shape=[jax.ShapeDtypeStr...]
    pallas_call x1, Pallas kernels: 171 us -> 167 us  [per_device(): pl.pallas_call(kernel, out_shape=[jax.ShapeDtypeStruct((ROWS, HEADS * DIM...]
where the time goes in v4:
time: 173 us; the launch traced here: 172 us
  Pallas kernels  172 us (99%)
    pallas_call x1, Pallas kernels, per_device(): pl.pallas_call(kernel, out_shape=[jax.ShapeDtypeStruct((ROWS, HEADS * DIM...  167 us
    pallas_call x1, Pallas kernels, per_device(): pl.pallas_call(finish_kernel, grid=(PARTS,), out_shape=[jax.ShapeDtypeStr...  4.32 us

profile of v4, /device:TPU:1, one launch (start us, length us, event | category | flops | bytes accessed | tf_op | source)
XLA Modules:
  0.0 172.4 jit_solution(11291593303448785543)
XLA Ops:
  0.6 167.4 %attention.1 = (bf16[384,1024]{1,0:T(8,128)(2,1)}, bf16[384,1024]{1,0:T(8,128)(2,1)}, bf16[384,1024]{1,0:T(8,128)(2,1)}, bf16[384,1024]{1,0:T(8,128)(2,1)}) custom-call(bf16[384,1024]{1,0:T(8,128)(2,1)} %q_ref.1, bf16[384,1024]{1,0:T(8,128)(2,1)} %k_ref.1, bf16[384,1024]{1,0:T(8,128)(2,1)} %v_ref.1, bf16[384,1024]{1,0:T(8,128)(2,1)} %g_ref.1, ...), custom_call_target="tpu_custom_call" | custom-call | tf_op jit(solution)/shard_map/attention/pallas_call | solution.py:427
  168.0 4.3 %finish.1 = (bf16[384,1024]{1,0:T(8,128)(2,1)}, bf16[384,1024]{1,0:T(8,128)(2,1)}, bf16[384,1024]{1,0:T(8,128)(2,1)}, bf16[384,1024]{1,0:T(8,128)(2,1)}) custom-call(bf16[384,1024]{1,0:T(8,128)(2,1)} %get-tuple-element.8.refs_0_, bf16[384,1024]{1,0:T(8,128)(2,1)} %get-tuple-element.9.refs_1_, bf16[384,1024]{1,0:T(8,128)(2,1)} %get-tuple-element.10.refs_2_, ...), custom_call_target="tpu_custom_call" | custom-call | tf_op jit(solution)/shard_map/finish/pallas_call | solution.py:456

commit v5 on v4

--- a/solution.py
+++ b/solution.py
@@ -21,7 +21,6 @@
 RUN = HALF // OWNED
 WINDOW = 6
 AHEAD = 6
-PARTS = 3
 ABSENT = 64.0
 NEG = -1e30
 SCALE = DIM ** -0.5
@@ -416,8 +415,16 @@
 
 
 def finish_kernel(*refs):
+    held, came, went = refs[8:]
+    ins = [pltpu.make_async_copy(refs[a], held.at[a], came.at[a]) for a in range(4)]
+    outs = [pltpu.make_async_copy(held.at[a], refs[4 + a], went.at[a]) for a in range(4)]
     for a in range(4):
-        refs[4 + a][...] = refs[a][...]
+        ins[a].start()
+    for a in range(4):
+        ins[a].wait()
+        outs[a].start()
+    for a in range(4):
+        outs[a].wait()
 
 
 def per_device(queries, keys, values, grad_out, cluster):
@@ -452,13 +459,13 @@
         ),
         name="attention",
     )(queries, keys, values, grad_out, labels, jnp.asarray(order, BF16), jnp.asarray(order.T, BF16))
-    spec = pl.BlockSpec((ROWS // PARTS, HEADS * DIM), lambda i: (i, 0))
     return pl.pallas_call(
         finish_kernel,
-        grid=(PARTS,),
         out_shape=[jax.ShapeDtypeStruct((ROWS, HEADS * DIM), BF16)] * 4,
-        in_specs=[spec] * 4,
-        out_specs=[spec] * 4,
+        in_specs=[pl.BlockSpec(memory_space=ANY)] * 4,
+        out_specs=[pl.BlockSpec(memory_space=ANY)] * 4,
+        scratch_shapes=[VMEM((4, ROWS, HEADS * DIM), BF16), dma((4,)), dma((4,))],
+        compiler_params=pltpu.CompilerParams(vmem_limit_bytes=60 * 2**20),
         name="finish",
     )(*outs)
 

time: 173 us -> 171 us (0.988)
  Pallas kernels: 172 us -> 170 us
where the time goes in v5:
time: 171 us
  Pallas kernels  170 us (99%)
    pallas_call x1, Pallas kernels, per_device(): pl.pallas_call(kernel, out_shape=[jax.ShapeDtypeStruct((ROWS, HEADS * DIM...  167 us

profile of v5, /device:TPU:1, one launch (start us, length us, event | category | flops | bytes accessed | tf_op | source)
XLA Modules:
  0.0 171.0 jit_solution(2257771470067154932)
XLA Ops:
  0.6 167.4 %attention.1 = (bf16[384,1024]{1,0:T(8,128)(2,1)}, bf16[384,1024]{1,0:T(8,128)(2,1)}, bf16[384,1024]{1,0:T(8,128)(2,1)}, bf16[384,1024]{1,0:T(8,128)(2,1)}) custom-call(bf16[384,1024]{1,0:T(8,128)(2,1)} %q_ref.1, bf16[384,1024]{1,0:T(8,128)(2,1)} %k_ref.1, bf16[384,1024]{1,0:T(8,128)(2,1)} %v_ref.1, bf16[384,1024]{1,0:T(8,128)(2,1)} %g_ref.1, ...), custom_call_target="tpu_custom_call" | custom-call | tf_op jit(solution)/shard_map/attention/pallas_call | solution.py:434
  168.0 2.9 %finish.1 = (bf16[384,1024]{1,0:T(8,128)(2,1)}, bf16[384,1024]{1,0:T(8,128)(2,1)}, bf16[384,1024]{1,0:T(8,128)(2,1)}, bf16[384,1024]{1,0:T(8,128)(2,1)}) custom-call(bf16[384,1024]{1,0:T(8,128)(2,1)} %get-tuple-element.8.refs_0_, bf16[384,1024]{1,0:T(8,128)(2,1)} %get-tuple-element.9.refs_1_, bf16[384,1024]{1,0:T(8,128)(2,1)} %get-tuple-element.10.refs_2_, ...), custom_call_target="tpu_custom_call" | custom-call | tf_op jit(solution)/shard_map/finish/pallas_call | solution.py:462

commit v6 on v5

--- a/solution.py
+++ b/solution.py
@@ -339,15 +339,14 @@
         return 0
 
     lax.fori_loop(0, OWNED, attend_one, 0)
-    lax.fori_loop(0, 3, spread, 0)
     lax.fori_loop(27, 29, pack, 0)
+    lax.fori_loop(0, 2, spread, 0)
+    lax.fori_loop(29, 31, pack, 0)
     deliver(0, 0)
     lax.fori_loop(25, 27, regroup, 0)
+    pack(31, 0)
+    lax.fori_loop(2, 5, spread, 0)
     deliver(1, 0)
-    lax.fori_loop(29, 31, pack, 0)
-    deliver(2, 0)
-    pack(31, 0)
-    lax.fori_loop(3, 5, spread, 0)
     lax.fori_loop(27, 32, regroup, 0)
 
     def value_one(j, _):
@@ -359,7 +358,7 @@
 
         @pl.when(j % 4 == 3)
         def _():
-            deliver(3 + j // 4, 0)
+            deliver(2 + j // 4, 0)
 
         return 0
 
@@ -368,7 +367,7 @@
 
     def behind(i, _):
         backward(x, y, top, inv, dk_acc, i)
-        deliver(i + 5, 0)
+        deliver(i + 4, 0)
 
         @pl.when(i < 6)
         def _():
@@ -377,7 +376,7 @@
         return 0
 
     lax.fori_loop(0, OWNED, behind, 0)
-    lax.fori_loop(16, 13 + AHEAD, spread, 0)
+    lax.fori_loop(16, 12 + AHEAD, spread, 0)
 
     def leave(n, _):
         @pl.when(n + AHEAD < 32)
@@ -387,7 +386,7 @@
         deliver(n, 0)
         return 0
 
-    lax.fori_loop(13, 32, leave, 0)
+    lax.fori_loop(12, 32, leave, 0)
 
     def drain(i, _):
         wait_for(zbuf.at[i], o_recv.at[i])

time: 171 us -> 172 us (level)
  no operation moved by 1% of the time
where the time goes in v6:
time: 172 us; the launch traced here: 171 us
  Pallas kernels  171 us (99%)
    pallas_call x1, Pallas kernels, per_device(): pl.pallas_call(kernel, out_shape=[jax.ShapeDtypeStruct((ROWS, HEADS * DIM...  168 us

profile of v6, /device:TPU:1, one launch (start us, length us, event | category | flops | bytes accessed | tf_op | source)
XLA Modules:
  0.0 171.4 jit_solution(17125490036024488780)
XLA Ops:
  0.6 167.8 %attention.1 = (bf16[384,1024]{1,0:T(8,128)(2,1)}, bf16[384,1024]{1,0:T(8,128)(2,1)}, bf16[384,1024]{1,0:T(8,128)(2,1)}, bf16[384,1024]{1,0:T(8,128)(2,1)}) custom-call(bf16[384,1024]{1,0:T(8,128)(2,1)} %q_ref.1, bf16[384,1024]{1,0:T(8,128)(2,1)} %k_ref.1, bf16[384,1024]{1,0:T(8,128)(2,1)} %v_ref.1, bf16[384,1024]{1,0:T(8,128)(2,1)} %g_ref.1, ...), custom_call_target="tpu_custom_call" | custom-call | tf_op jit(solution)/shard_map/attention/pallas_call | solution.py:433
  168.4 2.9 %finish.1 = (bf16[384,1024]{1,0:T(8,128)(2,1)}, bf16[384,1024]{1,0:T(8,128)(2,1)}, bf16[384,1024]{1,0:T(8,128)(2,1)}, bf16[384,1024]{1,0:T(8,128)(2,1)}) custom-call(bf16[384,1024]{1,0:T(8,128)(2,1)} %get-tuple-element.8.refs_0_, bf16[384,1024]{1,0:T(8,128)(2,1)} %get-tuple-element.9.refs_1_, bf16[384,1024]{1,0:T(8,128)(2,1)} %get-tuple-element.10.refs_2_, ...), custom_call_target="tpu_custom_call" | custom-call | tf_op jit(solution)/shard_map/finish/pallas_call | solution.py:461
